TPU v7x, 32 devices: a whole 2x2x4 slice. The times are simulated.
32 devices in a mesh: seq: 32 (over z, y, x, core).
Axes of the slice: x: 2, y: 2, z: 4, core: 2. Of those that a mesh axis runs over, the one named last changes fastest.
Arguments:
- tokens: bfloat16 [2, 16384, 1024], P(None, 'seq'), may hold values from -6 to 6
- seq_starts: int32 [2, 16384], P(None, 'seq'), may hold values from 0 to 15360, as said below
- seq_lengths: int32 [2, 16384], P(None, 'seq'), may hold values from 1 to 16384, as said below
- gain_in: float32 [1024], replicated, may hold values from 0.25 to 1.75
- gain_mlp: float32 [1024], replicated, may hold values from 0.25 to 1.75
- w_in: bfloat16 [1024, 3584], replicated, may hold values from -0.1875 to 0.1875
- w_out: bfloat16 [1024, 1024], replicated, may hold values from -0.1875 to 0.1875
- w_gate_up: bfloat16 [1024, 5632], replicated, may hold values from -0.1875 to 0.1875
- w_down: bfloat16 [2816, 1024], replicated, may hold values from -0.109375 to 0.109375
- cotangent: bfloat16 [2, 16384, 1024], P(None, 'seq'), may hold values from -6 to 6
Outputs:
- mixed_out: bfloat16 [2, 16384, 1024], P(None, 'seq')
- grad_tokens: float32 [2, 16384, 1024], P(None, 'seq')
- grad_gain_in: float32 [1024], P('seq')
- grad_gain_mlp: float32 [1024], P('seq')
- grad_w_in: float32 [1024, 3584], P('seq')
- grad_w_out: float32 [1024, 1024], P('seq')
- grad_w_gate_up: float32 [1024, 5632], P('seq')
- grad_w_down: float32 [2816, 1024], P('seq')
Inputs may be any that keep to these rules, and one draw needn't show every extreme that they name: `seq_starts`: tokens of one sequence occupy a run of positions beginning at this value, which never falls along a row and is a multiple of 64. Row 0 holds a single sequence filling the whole row. Every other row holds sequences of 1024 to 8192 tokens, each followed by padding up to a multiple of 64 positions, and ends with a sequence of exactly 1024 tokens that starts at 15360; the sequence before that one may be cut short. `seq_lengths`: the same for all tokens of a sequence; positions from start + length up to the next sequence's start are padding, fewer than 64 of them.
All inputs are finite; a program needn't handle non-finite values.
Results may differ from a plain program's by a relative error of at most 0.017.
Values may be sent and summed in bfloat16 or wider, within the bound.
A program may use at most 896 MiB of HBM per device.

v0:
```python
import jax
import jax.numpy as jnp
from jax import lax
from jax.sharding import PartitionSpec as P

HEADS = 16
FEAT = 16
WINDOW = 64


EPSILON = 1e-06
PRECISE = lax.Precision.HIGHEST


def passed_along(value, axis, steps):
    count = lax.axis_size(axis)
    initial, last = (max(0, -steps), min(count, count - steps))
    return lax.ppermute(value, axis, [(source, source + steps) for source in range(initial, last)])


def entering(shard, axis, join, neutral, backward):
    count = lax.axis_size(axis)
    place = lax.axis_index(axis)
    ahead = count - 1 - place if backward else place
    gathered = jax.tree.map(
        lambda a, kind: lax.all_gather(a.astype(kind), axis), shard, (jnp.bfloat16, jnp.bfloat16)
    )
    state = jax.tree.map(lambda a, e: jnp.zeros_like(a) + jnp.asarray(e, a.dtype), shard, neutral)

    def one(turn, state):
        source = count - 1 - turn if backward else turn
        return join(
            state,
            jax.tree.map(
                lambda a, own: lax.dynamic_index_in_dim(a, source, 0, False).astype(own.dtype),
                gathered,
                shard,
            ),
        )

    return lax.fori_loop(0, ahead, one, state)


def features(vectors):
    feat_width = vectors.shape[-1]
    outer_part = (vectors[..., :, None] * vectors[..., None, :]).reshape(
        vectors.shape[:-1] + (feat_width * feat_width,)
    )
    constant = jnp.ones(vectors.shape[:-1] + (1,), jnp.float32)
    return jnp.concatenate(
        [constant, vectors * feat_width ** (-0.25), outer_part * (2.0 * feat_width) ** (-0.5)],
        axis=-1,
    )


def features_back(vectors, gradient):
    feat_width = vectors.shape[-1]
    linear_part = gradient[..., 1 : 1 + feat_width] * feat_width ** (-0.25)
    square_part = gradient[..., 1 + feat_width :].reshape(
        gradient.shape[:-1] + (feat_width, feat_width)
    ) * (2.0 * feat_width) ** (-0.5)
    both_sides = square_part + jnp.swapaxes(square_part, -1, -2)
    return linear_part + jnp.einsum("...ab,...b->...a", both_sides, vectors, precision=PRECISE)


def chain(earlier, latter):
    state_a, flag_a = earlier
    state_b, flag_b = latter
    return (state_b + (1.0 - flag_b)[:, None, None, None] * state_a, jnp.maximum(flag_a, flag_b))


def linear_scores(q_lin, k_lin, inner_mask):
    scores = jnp.einsum(
        "ihf,jhf->hij", q_lin, k_lin, preferred_element_type=jnp.float32
    ) * FEAT ** (-0.5)
    weights = jnp.where(inner_mask[None], 1.0 + scores + 0.5 * scores * scores, 0.0)
    return (scores, weights)


def window_logits(q_win, keys_all, near_mask, head_size):
    logits = jnp.einsum(
        "ihe,jhe->hij", q_win, keys_all, preferred_element_type=jnp.float32
    ) * head_size ** (-0.5)
    return jnp.where(near_mask[None], logits, -1e30)


def shards(
    tokens, seq_starts, seq_lengths, gain_in, gain_mlp, w_in, w_out, w_gate_up, w_down, cotangent
):
    row_count, tok_count, model_width = tokens.shape
    head_size = model_width // HEADS
    lin_cols = HEADS * FEAT
    hidden_width = w_down.shape[0]
    block_begin = lax.axis_index("seq") * tok_count
    places = block_begin + jnp.arange(tok_count, dtype=jnp.int32)
    key_places = block_begin - WINDOW + jnp.arange(tok_count + WINDOW, dtype=jnp.int32)
    seq_ends = seq_starts + seq_lengths
    inner_mask = (seq_starts[:, :, None] <= places[None, None, :]) & (
        places[None, None, :] <= places[None, :, None]
    )
    inner_mask = inner_mask & (places[None, None, :] < seq_ends[:, :, None])
    near_mask = (seq_starts[:, :, None] <= key_places[None, None, :]) & (
        key_places[None, None, :] <= places[None, :, None]
    )
    near_mask = (
        near_mask
        & (key_places[None, None, :] >= places[None, :, None] - WINDOW)
        & (key_places[None, None, :] < seq_ends[:, :, None])
    )
    earlier_mask = (seq_starts < block_begin).astype(jnp.float32)[:, :, None, None]
    last_start = seq_starts[:, -1]
    owned_mask = ((seq_starts == last_start[:, None]) & (places[None, :] < seq_ends)).astype(
        jnp.float32
    )[:, :, None, None]
    reset_flag = (last_start >= block_begin).astype(jnp.float32)
    stream = tokens.astype(jnp.float32)
    scale_in = lax.rsqrt(jnp.mean(stream * stream, axis=-1, keepdims=True) + EPSILON)
    normed = (
        (stream * scale_in * gain_in)
        .astype(jnp.bfloat16)
        .reshape(row_count * tok_count, model_width)
    )
    projected = (
        jnp.dot(normed, w_in, preferred_element_type=jnp.float32)
        .astype(jnp.bfloat16)
        .reshape(row_count, tok_count, -1)
    )
    q_lin = projected[..., :lin_cols].reshape(row_count, tok_count, HEADS, FEAT)
    k_lin = projected[..., lin_cols : 2 * lin_cols].reshape(row_count, tok_count, HEADS, FEAT)
    q_win = projected[..., 2 * lin_cols : 2 * lin_cols + model_width]
    k_win = projected[..., 2 * lin_cols + model_width : 2 * lin_cols + 2 * model_width]
    values = projected[..., 2 * lin_cols + 2 * model_width :]
    kv_tails = jnp.stack([k_win[:, -WINDOW:], values[:, -WINDOW:]])
    halo_rows = passed_along(kv_tails, "seq", 1)
    keys_all = jnp.concatenate([halo_rows[0], k_win], axis=1).reshape(
        row_count, tok_count + WINDOW, HEADS, head_size
    )
    values_all = jnp.concatenate([halo_rows[1], values], axis=1).reshape(
        row_count, tok_count + WINDOW, HEADS, head_size
    )
    q_win = q_win.reshape(row_count, tok_count, HEADS, head_size)
    values = values.reshape(row_count, tok_count, HEADS, head_size)
    values_wide = values.astype(jnp.float32)
    key_feat = features(k_lin.astype(jnp.float32)) * owned_mask
    state_local = jnp.einsum("rjhp,rjhe->rhpe", key_feat, values_wide, precision=PRECISE)
    state_in, unused = entering(
        (state_local, reset_flag),
        "seq",
        chain,
        (jnp.zeros_like(state_local), jnp.zeros_like(reset_flag)),
        False,
    )
    local_rows, window_rows, total_rows = ([], [], [])
    for row_index in range(row_count):
        scores, weights = linear_scores(q_lin[row_index], k_lin[row_index], inner_mask[row_index])
        local_rows.append(
            jnp.einsum(
                "hij,jhe->ihe",
                weights.astype(jnp.bfloat16),
                values[row_index],
                preferred_element_type=jnp.float32,
            )
        )
        logits = window_logits(
            q_win[row_index], keys_all[row_index], near_mask[row_index], head_size
        )
        row_top = jnp.max(logits, axis=-1, keepdims=True)
        exponent = jnp.exp(logits - row_top)
        totals = jnp.sum(exponent, axis=-1, keepdims=True)
        attn_probs = exponent / totals
        window_rows.append(
            jnp.einsum(
                "hij,jhe->ihe",
                attn_probs.astype(jnp.bfloat16),
                values_all[row_index],
                preferred_element_type=jnp.float32,
            )
        )
        total_rows.append(row_top + jnp.log(totals))
    feat_q = features(q_lin.astype(jnp.float32)) * earlier_mask
    inter = jnp.einsum("rihp,rhpe->rihe", feat_q, state_in, precision=PRECISE)
    numerator = jnp.stack(local_rows) + inter
    rho = lax.rsqrt(jnp.mean(numerator * numerator, axis=-1, keepdims=True) + EPSILON)
    linear_out = numerator * rho
    windowed = jnp.stack(window_rows)
    mixed = (linear_out + windowed).astype(jnp.bfloat16).reshape(row_count * tok_count, model_width)
    resid = stream.reshape(row_count * tok_count, model_width) + jnp.dot(
        mixed, w_out, preferred_element_type=jnp.float32
    )
    scale_mlp = lax.rsqrt(jnp.mean(resid * resid, axis=-1, keepdims=True) + EPSILON)
    hnorm = (resid * scale_mlp * gain_mlp).astype(jnp.bfloat16)
    gate_up = jnp.dot(hnorm, w_gate_up, preferred_element_type=jnp.float32)
    gate_part = gate_up[:, :hidden_width]
    up_part = gate_up[:, hidden_width:]
    sigmoid_gate = jax.nn.sigmoid(gate_part)
    hidden = (gate_part * sigmoid_gate * up_part).astype(jnp.bfloat16)
    result = resid + jnp.dot(hidden, w_down, preferred_element_type=jnp.float32)
    mixed_out = result.astype(jnp.bfloat16).reshape(row_count, tok_count, model_width)
    grad_out = cotangent.reshape(row_count * tok_count, model_width)
    grad_down = jnp.dot(hidden.T, grad_out, preferred_element_type=jnp.float32)
    grad_hidden = jnp.dot(grad_out, w_down.T, preferred_element_type=jnp.float32)
    grad_gate = grad_hidden * up_part * sigmoid_gate * (1.0 + gate_part * (1.0 - sigmoid_gate))
    grad_up = grad_hidden * gate_part * sigmoid_gate
    grad_gu = jnp.concatenate([grad_gate, grad_up], axis=1).astype(jnp.bfloat16)
    grad_gate_up = jnp.dot(hnorm.T, grad_gu, preferred_element_type=jnp.float32)
    grad_hnorm = jnp.dot(grad_gu, w_gate_up.T, preferred_element_type=jnp.float32)
    grad_gain_mlp = jnp.sum(grad_hnorm * resid * scale_mlp, axis=0)
    scaled_mlp = grad_hnorm * gain_mlp
    grad_resid = grad_out.astype(jnp.float32) + scale_mlp * scaled_mlp
    grad_resid = grad_resid - resid * scale_mlp**3 * jnp.mean(
        scaled_mlp * resid, axis=-1, keepdims=True
    )
    grad_branch = grad_resid.astype(jnp.bfloat16)
    grad_out_w = jnp.dot(mixed.T, grad_branch, preferred_element_type=jnp.float32)
    grad_mixed = jnp.dot(grad_branch, w_out.T, preferred_element_type=jnp.float32).astype(
        jnp.bfloat16
    )
    grad_mixed = grad_mixed.reshape(row_count, tok_count, HEADS, head_size)
    grad_lin = grad_mixed.astype(jnp.float32)
    grad_numer = (
        rho * (grad_lin - linear_out * jnp.mean(grad_lin * linear_out, axis=-1, keepdims=True))
    ).astype(jnp.bfloat16)
    grad_numer_wide = grad_numer.astype(jnp.float32)
    grad_state_in = jnp.einsum("rihp,rihe->rhpe", feat_q, grad_numer_wide, precision=PRECISE)
    grad_state, unused = entering(
        (grad_state_in, reset_flag),
        "seq",
        chain,
        (jnp.zeros_like(grad_state_in), jnp.zeros_like(reset_flag)),
        True,
    )
    grad_feat_q = (
        jnp.einsum("rihe,rhpe->rihp", grad_numer_wide, state_in, precision=PRECISE) * earlier_mask
    )
    q_lin_rows, k_lin_rows, value_rows, q_win_rows, key_all_rows, value_all_rows = (
        [],
        [],
        [],
        [],
        [],
        [],
    )
    for row_index in range(row_count):
        scores, weights = linear_scores(q_lin[row_index], k_lin[row_index], inner_mask[row_index])
        grad_weights = jnp.einsum(
            "ihe,jhe->hij",
            grad_numer[row_index],
            values[row_index],
            preferred_element_type=jnp.float32,
        )
        grad_scores = jnp.where(
            inner_mask[row_index][None], grad_weights * (1.0 + scores), 0.0
        ).astype(jnp.bfloat16)
        q_lin_rows.append(
            jnp.einsum(
                "hij,jhf->ihf", grad_scores, k_lin[row_index], preferred_element_type=jnp.float32
            )
            * FEAT ** (-0.5)
        )
        k_lin_rows.append(
            jnp.einsum(
                "hij,ihf->jhf", grad_scores, q_lin[row_index], preferred_element_type=jnp.float32
            )
            * FEAT ** (-0.5)
        )
        value_rows.append(
            jnp.einsum(
                "hij,ihe->jhe",
                weights.astype(jnp.bfloat16),
                grad_numer[row_index],
                preferred_element_type=jnp.float32,
            )
        )
        logits = window_logits(
            q_win[row_index], keys_all[row_index], near_mask[row_index], head_size
        )
        attn_probs = jnp.exp(logits - total_rows[row_index])
        grad_probs = jnp.einsum(
            "ihe,jhe->hij",
            grad_mixed[row_index],
            values_all[row_index],
            preferred_element_type=jnp.float32,
        )
        grad_logits = attn_probs * (
            grad_probs - jnp.sum(attn_probs * grad_probs, axis=-1, keepdims=True)
        )
        grad_logits = grad_logits.astype(jnp.bfloat16)
        q_win_rows.append(
            jnp.einsum(
                "hij,jhe->ihe", grad_logits, keys_all[row_index], preferred_element_type=jnp.float32
            )
            * head_size ** (-0.5)
        )
        key_all_rows.append(
            jnp.einsum(
                "hij,ihe->jhe", grad_logits, q_win[row_index], preferred_element_type=jnp.float32
            )
            * head_size ** (-0.5)
        )
        value_all_rows.append(
            jnp.einsum(
                "hij,ihe->jhe",
                attn_probs.astype(jnp.bfloat16),
                grad_mixed[row_index],
                preferred_element_type=jnp.float32,
            )
        )
    grad_keys_all = jnp.stack(key_all_rows).reshape(row_count, tok_count + WINDOW, model_width)
    grad_values_all = jnp.stack(value_all_rows).reshape(row_count, tok_count + WINDOW, model_width)
    returned_rows = jnp.stack([grad_keys_all[:, :WINDOW], grad_values_all[:, :WINDOW]])
    returned_rows = passed_along(returned_rows.astype(jnp.bfloat16), "seq", -1).astype(
        returned_rows.dtype
    )
    filler = jnp.zeros((2, row_count, tok_count - WINDOW, model_width), jnp.float32)
    returned_rows = jnp.concatenate([filler, returned_rows], axis=2)
    grad_key_feat = (
        jnp.einsum("rjhe,rhpe->rjhp", values_wide, grad_state, precision=PRECISE) * owned_mask
    )
    grad_values_state = jnp.einsum("rjhp,rhpe->rjhe", key_feat, grad_state, precision=PRECISE)
    grad_q_lin = jnp.stack(q_lin_rows) + features_back(q_lin.astype(jnp.float32), grad_feat_q)
    grad_k_lin = jnp.stack(k_lin_rows) + features_back(k_lin.astype(jnp.float32), grad_key_feat)
    grad_q_win = jnp.stack(q_win_rows).reshape(row_count, tok_count, model_width)
    grad_k_win = grad_keys_all[:, WINDOW:] + returned_rows[0]
    grad_values = (jnp.stack(value_rows) + grad_values_state).reshape(
        row_count, tok_count, model_width
    )
    grad_values = grad_values + grad_values_all[:, WINDOW:] + returned_rows[1]
    grad_projected = jnp.concatenate(
        [
            grad_q_lin.reshape(row_count, tok_count, lin_cols),
            grad_k_lin.reshape(row_count, tok_count, lin_cols),
            grad_q_win,
            grad_k_win,
            grad_values,
        ],
        axis=-1,
    )
    grad_projected = grad_projected.astype(jnp.bfloat16).reshape(row_count * tok_count, -1)
    grad_in_w = jnp.dot(normed.T, grad_projected, preferred_element_type=jnp.float32)
    grad_normed = jnp.dot(grad_projected, w_in.T, preferred_element_type=jnp.float32).reshape(
        row_count, tok_count, model_width
    )
    grad_gain_in = jnp.sum(
        (grad_normed * stream * scale_in).reshape(row_count * tok_count, model_width), axis=0
    )
    scaled_in = grad_normed * gain_in
    grad_tokens = grad_resid.reshape(row_count, tok_count, model_width) + scale_in * scaled_in
    grad_tokens = grad_tokens - stream * scale_in**3 * jnp.mean(
        scaled_in * stream, axis=-1, keepdims=True
    )
    part_in, part_out, part_gate_up, part_down, part_gain_in, part_gain_mlp = (
        lax.psum_scatter(grad_in_w, "seq", scatter_dimension=0, tiled=True),
        lax.psum_scatter(grad_out_w, "seq", scatter_dimension=0, tiled=True),
        lax.psum_scatter(grad_gate_up, "seq", scatter_dimension=0, tiled=True),
        lax.psum_scatter(grad_down, "seq", scatter_dimension=0, tiled=True),
        lax.psum_scatter(grad_gain_in, "seq", scatter_dimension=0, tiled=True),
        lax.psum_scatter(grad_gain_mlp, "seq", scatter_dimension=0, tiled=True),
    )
    return (
        mixed_out,
        grad_tokens,
        part_gain_in,
        part_gain_mlp,
        part_in,
        part_out,
        part_gate_up,
        part_down,
    )


def solution(mesh):
    placed = (
        P(None, "seq", None),
        P(None, "seq"),
        P(None, "seq"),
        P(),
        P(),
        P(),
        P(),
        P(),
        P(),
        P(None, "seq", None),
    )
    return jax.shard_map(
        shards,
        mesh=mesh,
        in_specs=placed,
        out_specs=(
            P(None, "seq", None),
            P(None, "seq", None),
            P("seq"),
            P("seq"),
            P("seq", None),
            P("seq", None),
            P("seq", None),
            P("seq", None),
        ),
        check_vma=False,
    )
```

profile of v0, /device:TPU:0, one launch (start us, length us, event | category | flops | bytes accessed | tf_op | source)
XLA Modules:
  0.0 1873.2 jit_solution(47579288749086959)
XLA Ops:
  12.2 12.1 convolution_convert_fusion
  33.6 9.0 multiply_multiply_fusion.1
  47.3 17.1 fusion.51
  87.5 8.2 fusion.92
  95.7 8.2 fusion.91
  103.9 8.4 multiply_multiply_fusion
  112.3 9.2 convolution_bitcast_fusion.3
  130.8 46.6 %all-reduce.1 = bf16[64]{0:T(256)(128)(2,1)S(1)} all-reduce(bf16[64]{0:T(256)(128)(2,1)S(1)} %dynamic-update-slice), channel_id=3, replica_groups=mesh['seq'=32] {'seq'}, use_global_device_ids=true, to_apply=%add.1 | all-reduce | flops 64 | bytes 256
  196.9 14.5 fusion.90
  211.4 8.4 fusion.89
  219.8 9.5 fusion.6
  229.3 9.3 fusion.7
  238.6 9.3 fusion.54
  247.9 9.2 fusion.53
  257.0 86.6 %all-gather.6.cloned.1.call-done = bf16[64,16,273,64]{2,3,1,0:T(8,128)(2,1)} async-done(((bf16[2,16,273,64]{2,3,1,0:T(8,128)(2,1)}), bf16[64,16,273,64]{2,3,1,0:T(8,128)(2,1)}) %all-gather.6.cloned.1.call-update) | async-done | bytes 35782672 | tf_op jit(solution)/shard_map/all_gather | solution.py:26
  347.3 26.6 %multiply_reduce_fusion.6 = (f32[2,512,16]{1,2,0:T(8,128)S(1)}, f32[2,512,16,64]{1,3,2,0:T(8,128)}) fusion(f32[2,16,273,64]{3,2,1,0:T(8,128)} %get-tuple-element.136, f32[2,512,16,256]{1,3,2,0:T(8,128)} %bitcast.276, f32[2,512,16,16]{1,3,2,0:T(8,128)S(1)} %copy-done.31, f32[273]{0:T(512)S(1)} %pad.29.clone, f32[2,512]{1,0:T(2,128)S(1)} %get-tuple-element.229, ...), kind=kOutput, calls=%fused_computation.111 | convolution fusion | flops 3452731392 | bytes 28521540 | tf_op jit(solution)/shard_map/rihp,rhpe->rihe/dot_general | solution.py:181
  384.1 20.8 %fusion.83 = f32[1024,5632]{1,0:T(8,128)} fusion(bf16[1024,5632]{1,0:T(8,128)(2,1)} %param.21, f32[1024,1024]{1,0:T(8,128)S(1)} %get-tuple-element.239, f32[1024]{0:T(1024)S(1)} %copy-done.78, f32[1024]{0:T(1024)S(1)} %get-tuple-element.228), kind=kOutput, calls=%fused_computation.209 | convolution fusion | flops 11814305792 | bytes 38805504 | tf_op jit(solution)/shard_map/dot_general | solution.py:192
  404.9 21.8 %multiply_convert_fusion.3 = (bf16[1024,2816]{1,0:T(8,128)(2,1)}, bf16[1024,2816]{1,0:T(8,128)(2,1)}, bf16[1024,2816]{1,0:T(8,128)(2,1)}) fusion(f32[1024,5632]{1,0:T(8,128)} %fusion.83, bf16[1024,1024]{1,0:T(8,128)(2,1)} %bitcast.331, bf16[2816,1024]{1,0:T(8,128)(2,1)} %param.22), kind=kOutput, calls=%fused_computation.48 | convolution fusion | flops 5951717376 | bytes 48234496 | tf_op jit(solution)/shard_map/dot_general | solution.py:201
  426.7 22.2 %multiply_reduce_fusion.2 = (f32[1024]{0:T(1024)}, f32[1024]{0:T(1024)S(1)}, f32[1024,1024]{1,0:T(8,128)}) fusion(f32[1024,1024]{1,0:T(8,128)} %copy-done.34, f32[1024]{0:T(1024)S(1)} %get-tuple-element.228, f32[1024]{0:T(1024)S(1)} %copy-done.78, bf16[1024,5632]{1,0:T(8,128)(2,1)} %param.21, bf16[1024,2816]{1,0:T(8,128)(2,1)} %get-tuple-element.197, ...), kind=kOutput, calls=%fused_computation.102 | convolution fusion | flops 11840518144 | bytes 31473664 | tf_op jit(solution)/shard_map/dot_general | solution.py:206
  459.3 6.8 reshape.400
  473.6 16.8 fusion.52
  490.5 7.2 fusion.67
  497.7 12.3 fusion.93
  510.1 21.8 %fusion.30 = f32[1024,5632]{1,0:T(8,128)} fusion(bf16[1024,2816]{1,0:T(8,128)(2,1)} %get-tuple-element.197, bf16[1024,2816]{1,0:T(8,128)(2,1)} %get-tuple-element.196, f32[1024,1024]{1,0:T(8,128)} %copy-done.34, f32[1024]{0:T(1024)S(1)} %copy-done.78, f32[1024]{0:T(1024)S(1)} %get-tuple-element.228), kind=kOutput, calls=%fused_computation.67 | convolution fusion | flops 11837374464 | bytes 38805504 | tf_op jit(solution)/shard_map/dot_general | solution.py:205
  534.4 12.8 multiply_reduce_fusion.1
  547.2 13.6 multiply_convert_fusion.1
  568.6 12.4 multiply_reduce_fusion
  581.0 13.5 multiply_convert_fusion
  602.5 11.1 fusion.16
  616.8 10.8 fusion.14
  635.6 6.5 multiply_convert_fusion.8
  644.8 6.5 multiply_convert_fusion.7
  653.6 9.9 select_convert_fusion.1
  663.6 6.6 fusion.55
  670.2 9.7 select_convert_fusion
  685.6 10.4 multiply_bitcast_fusion.1
  696.0 7.2 slice_multiply_fusion.1
  703.3 15.9 fusion.5
  727.8 9.3 convolution_bitcast_fusion.1
  749.4 399.4 %all-gather.8.cloned.1.call-done = bf16[64,16,273,64]{2,3,1,0:T(8,128)(2,1)} async-done(((bf16[2,16,273,64]{2,3,1,0:T(8,128)(2,1)}), bf16[64,16,273,64]{2,3,1,0:T(8,128)(2,1)}) %all-gather.8.cloned.1.call-update) | async-done | bytes 35782672 | tf_op jit(solution)/shard_map/all_gather | solution.py:26
  1151.3 333.7 %while.27 = (s32[]{:T(128)}, f32[2,16,273,64]{3,2,1,0:T(8,128)}, s32[]{:T(128)}, bf16[32,2,16,273,64]{3,4,2,1,0:T(8,128)(2,1)}, bf16[32,2]{1,0:T(8,128)(2,1)}, /*index=5*/s32[]{:T(128)}, s32[]{:T(128)}, s32[]{:T(128)}, s32[]{:T(128)}) while((s32[]{:T(128)}, f32[2,16,273,64]{3,2,1,0:T(8,128)}, s32[]{:T(128)}, ...), condition=%wide.region_12.13_spmd, body=%wide.region_11.12_spmd.sunk | while | flops 1677322 | bytes 10064039 | solution.py:41
  1210.1 5.7 convert_add_fusion.5
  1253.0 5.7 convert_add_fusion.5
  1306.6 5.7 convert_add_fusion.5
  1317.4 5.8 convert_add_fusion.5
  1328.2 5.8 convert_add_fusion.5
  1339.1 5.7 convert_add_fusion.5
  1382.2 5.7 convert_add_fusion.5
  1392.9 5.8 convert_add_fusion.5
  1403.8 5.8 convert_add_fusion.5
  1468.4 5.7 convert_add_fusion.5
  1479.2 5.7 convert_add_fusion.5
  1485.0 26.4 %maximum_add_fusion.2 = f32[2,512,16,64]{1,3,2,0:T(8,128)} fusion(f32[1,512,16,64]{1,3,2,0:T(8,128)} %convolution_bitcast_fusion.1, f32[1,512,16,64]{1,3,2,0:T(8,128)} %convolution_bitcast_fusion.2, f32[2,16,273,64]{3,2,1,0:T(8,128)} %get-tuple-element.137, f32[2,512,16,256]{1,3,2,0:T(8,128)} %bitcast.273, f32[2,512,16,16]{1,3,2,0:T(8,128)S(1)} %copy-done.30, ...), kind=kOutput, calls=%fused_computation.100 | convolution fusion | flops 3450650624 | bytes 28456004 | tf_op jit(solution)/shard_map/rjhp,rhpe->rjhe/dot_general | solution.py:319
  1516.9 10.2 multiply_bitcast_fusion
  1527.1 6.5 slice_multiply_fusion
  1533.6 26.1 %fusion.2 = f32[2,512,16,16]{1,3,2,0:T(8,128)S(1)} fusion(f32[2,512,16,16,16]{1,4,3,2,0:T(8,128)} %bitcast.279, f32[2,512,16,16]{1,3,2,0:T(8,128)S(1)} %copy-done.18), kind=kLoop, calls=%fused_computation.27 | loop fusion | flops 12320768 | bytes 18874368 | tf_op jit(solution)/shard_map/...ab,...b->...a/dot_general | solution.py:63
  1564.7 6.1 fusion.50
  1577.3 14.2 convolution_bitcast_fusion
  1591.6 11.7 add_convert_fusion
  1603.3 14.2 fusion.44
  1617.5 40.4 %all-reduce.4 = (f32[1024]{0:T(1024)S(1)}, f32[1024]{0:T(1024)S(1)}) all-reduce(f32[1024]{0:T(1024)S(1)} %get-tuple-element.170, f32[1024]{0:T(1024)S(1)} %copy-done.79), channel_id=5, replica_groups=mesh['seq'=32] {'seq'}, use_global_device_ids=true, to_apply=%region_17.18.clone | all-reduce | flops 2048 | bytes 16384
  1659.0 6.2 fusion.41
  1665.2 31.1 %reduce-scatter.9.cloned.1.call-done = f32[32,5632]{1,0:T(8,128)} async-done(((f32[1024,5632]{1,0:T(8,128)}), f32[32,5632]{1,0:T(8,128)}) %reduce-scatter.9.cloned.1.call-update) | async-done | bytes 720912 | tf_op jit(solution)/shard_map/reduce_scatter | solution.py:354
  1696.3 169.8 %reduce-scatter.5.cloned.1.call-done = f32[32,3584]{1,0:T(8,128)} async-done(((f32[1024,3584]{1,0:T(8,128)}), f32[32,3584]{1,0:T(8,128)}) %reduce-scatter.5.cloned.1.call-update) | async-done | bytes 458768 | tf_op jit(solution)/shard_map/reduce_scatter | solution.py:352
  (409 shorter events, 454.0 us)
Async XLA Ops:
  7.2 374.1 %copy-start = (bf16[1024,1024]{1,0:T(8,128)(2,1)S(1)}, bf16[1024,1024]{1,0:T(8,128)(2,1)}, u32[]{:S(2)}) copy-start(bf16[1024,1024]{1,0:T(8,128)(2,1)} %param.20) | copy-start | bytes 6291460
  7.2 336.4 %all-gather.6.cloned.1.call-start = ((), (), s32[]{:S(2)}) async-start(), calls=%async_computation.8 | async-start | bytes 51904512 | tf_op jit(solution)/shard_map/all_gather | solution.py:26
  12.2 12.1 copy-start.49
  30.9 11.8 copy-start.17
  33.6 13.0 copy-start.80
  46.6 427.0 %copy-start.70 = (f32[273]{0:T(512)}, f32[273]{0:T(512)S(1)}, u32[]{:S(2)}) copy-start(f32[273]{0:T(512)S(1)} %pad.29.clone) | copy-start | bytes 3280
  46.7 426.9 %copy-start.68 = (f32[2,512]{1,0:T(2,128)}, f32[2,512]{1,0:T(2,128)S(1)}, u32[]{:S(2)}) copy-start(f32[2,512]{1,0:T(2,128)S(1)} %get-tuple-element.229) | copy-start | bytes 12292
  64.4 1084.4 %all-gather.8.cloned.1.call-start = ((), (), s32[]{:S(2)}) async-start(), calls=%async_computation.9 | async-start | bytes 51904512 | tf_op jit(solution)/shard_map/all_gather | solution.py:26
  66.6 117.7 %collective-permute-start = (bf16[2,2,64,1024]{3,2,1,0:T(8,128)(2,1)}, bf16[2,2,64,1024]{3,2,1,0:T(8,128)(2,1)}, u32[]{:S(2)}, u32[]{:S(2)}) collective-permute-start(bf16[2,2,64,1024]{3,2,1,0:T(8,128)(2,1)} %pad_maximum_fusion.7), channel_id=1, source_target_pairs={{0,1},{1,2},{2,3},{3,4},{4,5},{5,6},{6,7},{7,8},{8,9},{9,10},{10,1... | collective-permute-start | bytes 1572872 | tf_op jit(solution)/shard_map/ppermute | solution.py:18
  72.0 15.5 copy-start.38
  87.3 25.0 %copy-start.55 = (pred[512,512]{1,0:T(8,128)(4,1)}, pred[512,512]{1,0:T(8,128)(4,1)S(1)}, u32[]{:S(2)}) copy-start(pred[512,512]{1,0:T(8,128)(4,1)S(1)} %get-tuple-element.222) | copy-start | bytes 786436
  87.3 34.2 %copy-start.53 = (pred[512,512]{1,0:T(8,128)(4,1)}, pred[512,512]{1,0:T(8,128)(4,1)S(1)}, u32[]{:S(2)}) copy-start(pred[512,512]{1,0:T(8,128)(4,1)S(1)} %get-tuple-element.221) | copy-start | bytes 786436
  87.4 16.5 copy-start.19
  87.5 8.2 copy-start.40
  87.5 8.2 copy-start.44
  103.9 8.4 copy-start.35
  112.3 12.2 copy-start.4
  112.3 12.4 copy-start.37
  194.0 17.4 copy-start.14
  196.9 14.5 copy-start.24
  196.9 14.5 copy-start.52
  211.3 27.2 %copy-start.58 = (f32[16,512]{1,0:T(8,128)}, f32[16,512]{1,0:T(8,128)S(1)}, u32[]{:S(2)}) copy-start(f32[16,512]{1,0:T(8,128)S(1)} %get-tuple-element.234) | copy-start | bytes 98308
  219.8 28.1 %copy-start.60 = (f32[16,512]{1,0:T(8,128)}, f32[16,512]{1,0:T(8,128)S(1)}, u32[]{:S(2)}) copy-start(f32[16,512]{1,0:T(8,128)S(1)} %get-tuple-element.232) | copy-start | bytes 98308
  229.3 9.3 copy-start.64
  229.3 9.3 copy-start.29
  238.6 9.3 copy-start.62
  238.6 9.3 copy-start.28
  346.0 27.8 %copy-start.77 = (bf16[32,2]{1,0:T(8,128)(2,1)}, bf16[32,2]{1,0:T(8,128)(2,1)S(1)}, u32[]{:S(2)}) copy-start(bf16[32,2]{1,0:T(8,128)(2,1)S(1)} %get-tuple-element.385) | copy-start | bytes 388
  384.1 20.8 %copy-start.34 = (f32[1024,1024]{1,0:T(8,128)}, f32[1024,1024]{1,0:T(8,128)S(1)}, u32[]{:S(2)}) copy-start(f32[1024,1024]{1,0:T(8,128)S(1)} %get-tuple-element.239) | copy-start | bytes 12582916
  490.4 1174.8 %reduce-scatter.7.cloned.1.call-start = ((), (), s32[]{:S(2)}) async-start(), calls=%async_computation.5 | async-start | bytes 4325376 | tf_op jit(solution)/shard_map/reduce_scatter | solution.py:353
  497.6 1167.6 %reduce-scatter.11.cloned.1.call-start = ((), (), s32[]{:S(2)}) async-start(), calls=%async_computation.7 | async-start | bytes 11894784 | tf_op jit(solution)/shard_map/reduce_scatter | solution.py:355
  510.0 1186.3 %reduce-scatter.9.cloned.1.call-start = ((), (), s32[]{:S(2)}) async-start(), calls=%async_computation.6 | async-start | bytes 23789568 | tf_op jit(solution)/shard_map/reduce_scatter | solution.py:354
  531.9 1334.2 %reduce-scatter.5.cloned.1.call-start = ((), (), s32[]{:S(2)}) async-start(), calls=%async_computation.4 | async-start | bytes 15138816 | tf_op jit(solution)/shard_map/reduce_scatter | solution.py:352
  534.3 12.8 copy-start.23
  547.2 13.6 copy-start.26
  581.0 13.6 copy-start.25
  634.2 10.6 copy-start.15
  634.2 109.9 %collective-permute-start.1 = (bf16[2,2,64,1024]{3,2,1,0:T(8,128)(2,1)}, bf16[2,2,64,1024]{3,2,1,0:T(8,128)(2,1)}, u32[]{:S(2)}, u32[]{:S(2)}) collective-permute-start(bf16[2,2,64,1024]{3,2,1,0:T(8,128)(2,1)} %pad_maximum_fusion.8), channel_id=1, source_target_pairs={{1,0},{2,1},{3,2},{4,3},{5,4},{6,5},{7,6},{8,7},{9,8},{10,9},{11,1... | collective-permute-start | bytes 1572872 | tf_op jit(solution)/shard_map/ppermute | solution.py:18
  653.6 9.9 copy-start.45
  663.5 6.6 copy-start.56
  663.5 22.0 %slice-start = ((s8[4587520]{0:T(1024)(128)(4,1)}), s8[4194304]{0:T(1024)(128)(4,1)S(1)}, s32[]{:S(2)}) async-start(s8[4587520]{0:T(1024)(128)(4,1)} %bitcast.268), calls=%async_computation.10 | async-start | bytes 8388608
  670.2 9.7 copy-start.43
  670.2 15.4 slice-start.1
  696.0 7.3 copy-start.20
  703.3 15.9 copy-start.48
  722.2 14.9 slice-start.4
  722.2 14.9 slice-start.5
  727.8 9.3 slice-start.6
  727.8 9.3 slice-start.7
  727.8 9.3 copy-start.54
  727.8 14.3 slice-start.2
  1151.3 333.7 %copy-start.30 = (f32[2,512,16,16]{1,3,2,0:T(8,128)S(1)}, f32[2,512,16,16]{1,3,2,0:T(8,128)}, u32[]{:S(2)}) copy-start(f32[2,512,16,16]{1,3,2,0:T(8,128)} %broadcast_multiply_fusion.1) | copy-start | bytes 3145732
  1151.3 333.7 %copy-start.67 = (f32[2,512]{1,0:T(2,128)S(1)}, f32[2,512]{1,0:T(2,128)}, u32[]{:S(2)}) copy-start(f32[2,512]{1,0:T(2,128)} %copy-done.66) | copy-start | bytes 12292
  1151.3 333.7 %copy-start.71 = (f32[273]{0:T(512)S(1)}, f32[273]{0:T(512)}, u32[]{:S(2)}) copy-start(f32[273]{0:T(512)} %copy-done.70) | copy-start | bytes 3280
  1533.6 26.1 %copy-start.46 = (f32[1,512,16,16]{1,3,2,0:T(8,128)S(1)}, f32[1,512,16,16]{1,3,2,0:T(8,128)}, u32[]{:S(2)}) copy-start(f32[1,512,16,16]{1,3,2,0:T(8,128)} %fusion.57) | copy-start | bytes 1572868
  1533.6 26.1 %copy-start.47 = (f32[1,512,16,16]{1,3,2,0:T(8,128)S(1)}, f32[1,512,16,16]{1,3,2,0:T(8,128)}, u32[]{:S(2)}) copy-start(f32[1,512,16,16]{1,3,2,0:T(8,128)} %fusion.58) | copy-start | bytes 1572868
  1563.1 7.7 slice-start.8
  1564.7 7.6 copy-start.10
  1591.6 11.7 copy-start.12
  1591.6 11.7 copy-start.74
  1591.6 11.7 copy-start.76
  1603.3 14.2 copy-start.79
  1603.3 55.7 %copy-start.75 = (f32[2,512]{1,0:T(2,128)S(1)}, f32[2,512]{1,0:T(2,128)}, u32[]{:S(2)}) copy-start(f32[2,512]{1,0:T(2,128)} %get-tuple-element.225) | copy-start | bytes 12292
  1659.0 207.1 %copy-start.1 = (bf16[1024,1024]{1,0:T(8,128)(2,1)S(1)}, bf16[1024,1024]{1,0:T(8,128)(2,1)}, u32[]{:S(2)}) copy-start(bf16[1024,1024]{1,0:T(8,128)(2,1)} %param.20) | copy-start | bytes 6291460
  (35 other events, 131.5 us)
Sparse Core Ops, SparseCore 0:
  64.6 279.0 all-gather.5
  490.5 658.2 all-gather.7
  1151.7 144.8 reduce-scatter.6
  1299.4 150.4 reduce-scatter.10
  1452.6 243.6 reduce-scatter.8
  1699.0 167.0 reduce-scatter.4
where the time goes:
time: 1890 us; the launch traced here: 1870 us
  waiting for transfers between devices  687 us (36%)
  matrix products  467 us (25%)
  other arithmetic  379 us (20%)
  local copies, waits for them, and re-layouts  233 us (12%)
  blocking collectives  86.9 us (5%)
    all_gather x2, waiting for transfers between devices, entering(): lax.all_gather(a.astype(kind), axis)  486 us
    add x31, other arithmetic, chain(): state_b + (1.0 - flag_b)[:, None, None, None] * state_a  177 us
    reduce_scatter x1, waiting for transfers between devices, shards(): lax.psum_scatter(grad_in_w, 'seq', scatter_dimension=0, tiled=True)  170 us
    dynamic_slice x62, local copies, waits for them, and re-layouts, one(): lax.dynamic_index_in_dim(a, source, 0, False).astype(own.dtype)  136 us
    unnamed x2, blocking collectives  86.9 us
    dot_general x2, other arithmetic, features_back(): jnp.einsum('...ab,...b->...a', both_sides, vectors, precision=PRECISE)  42 us
  transfers between devices with their start and end apart: 8, of which 4 were waited for; matrix products, arithmetic and copies ran while one was open for 46% of the time, Pallas kernels for 0%

commit v1 on v0

v1 whole, which is shorter than its diff:
```python
import functools
import jax
import jax.numpy as jnp
from jax import lax
from jax.experimental import pallas as pl
from jax.experimental.pallas import tpu as pltpu
from jax.sharding import PartitionSpec as P
F32=jnp.float32; BF=jnp.bfloat16
EPSILON=1e-6
MIB=1<<20

def nn(a,b): return lax.dot_general(a,b,(((1,),(0,)),((),())),preferred_element_type=F32)
def nt(a,b): return lax.dot_general(a,b,(((1,),(1,)),((),())),preferred_element_type=F32)
def tn(a,b): return lax.dot_general(a,b,(((0,),(0,)),((),())),preferred_element_type=F32)

def mlp_kernel(core_ref, mixed, tokens, cot, w_out, gain, wg, wu, wd,
               result, grad_resid, grad_mixed, gain_part, keep_gu, send_gu, keep_d, send_d, keep_o, send_o,
               resid, acc, dh, hn, hn_t, hid, dgate, dup, *, steps, chunk):
    step = pl.program_id(0)
    toks = mixed.shape[0]
    width = mixed.shape[1]
    count = toks // chunk
    first = core_ref[0] == 0

    def rows(n):
        return pl.ds(pl.multiple_of(n * chunk, chunk), chunk)

    @pl.when(step == 0)
    def _():
        def one(n, carry):
            r = rows(n)
            res = tokens[r, :].astype(F32) + nn(mixed[r, :], w_out[...])
            scale = lax.rsqrt(jnp.mean(res * res, axis=-1, keepdims=True) + EPSILON)
            h = (res * scale * gain[...]).astype(BF)
            resid[r, :] = res
            acc[r, :] = res
            dh[r, :] = jnp.zeros((chunk, width), F32)
            hn[r, :] = h
            return carry
        lax.fori_loop(0, count, one, 0)
        for n in range(count):
            hn_t[:, n * chunk:(n + 1) * chunk] = hn[n * chunk:(n + 1) * chunk, :].T

    def forward(n, carry):
        r = rows(n)
        h = hn[r, :]
        gate = nn(h, wg[...])
        up = nn(h, wu[...])
        dhid = nt(cot[r, :], wd[...])
        sig = 1.0 / (1.0 + jnp.exp(-gate))
        silu = gate * sig
        hidden = (silu * up).astype(BF)
        d_gate = (dhid * up * (sig + silu * (1.0 - sig))).astype(BF)
        d_up = (dhid * silu).astype(BF)
        hid[r, :] = hidden
        dgate[r, :] = d_gate
        dup[r, :] = d_up
        acc[r, :] += nn(hidden, wd[...])
        dh[r, :] += nt(d_gate, wg[...]) + nt(d_up, wu[...])
        return carry
    lax.fori_loop(0, count, forward, 0, unroll=2)

    half = width // 2
    grad_d = tn(hid[...], cot[...])
    left, right = grad_d[:, :half].astype(BF), grad_d[:, half:].astype(BF)
    keep_d[...] = jnp.where(first, left, right)
    send_d[...] = jnp.where(first, right, left)

    def weights(n, carry):
        r = rows(n)
        gg = nn(hn_t[r, :], dgate[...]).astype(BF)
        gu = nn(hn_t[r, :], dup[...]).astype(BF)
        keep_gu[r, :] = jnp.where(first, gg, gu)
        send_gu[r, :] = jnp.where(first, gu, gg)
        return carry
    lax.fori_loop(0, width // chunk, weights, 0, unroll=2)

    @pl.when(step == steps - 1)
    def _():
        gain_part[...] = jnp.zeros_like(gain_part)
        def one(n, carry):
            r = rows(n)
            res = resid[r, :]
            scale = lax.rsqrt(jnp.mean(res * res, axis=-1, keepdims=True) + EPSILON)
            grad = dh[r, :]
            gain_part[...] += jnp.sum(grad * res * scale, axis=0, keepdims=True)
            c = grad * gain[...]
            back = cot[r, :].astype(F32) + scale * c - res * (scale * scale * scale * jnp.mean(c * res, axis=-1, keepdims=True))
            result[r, :] = acc[r, :].astype(BF)
            grad_resid[r, :] = back
            b = back.astype(BF)
            hn[r, :] = b
            grad_mixed[r, :] = nt(b, w_out[...]).astype(BF)
            return carry
        lax.fori_loop(0, count, one, 0)
        for n in range(count):
            hn_t[:, n * chunk:(n + 1) * chunk] = mixed[n * chunk:(n + 1) * chunk, :].T
        def outer(n, carry):
            r = rows(n)
            go = nn(hn_t[r, :], hn[...])
            l, rr = go[:, :half].astype(BF), go[:, half:].astype(BF)
            keep_o[r, :] = jnp.where(first, l, rr)
            send_o[r, :] = jnp.where(first, rr, l)
            return carry
        lax.fori_loop(0, width // chunk, outer, 0)

def mlp(core, mixed, tokens, cot, w_out, gain, w_gate_up, w_down, tile=256, chunk=256):
    toks, width = mixed.shape
    ff = w_down.shape[0]
    steps = ff // tile
    half = width // 2
    whole = lambda s, c: (0, 0)
    one = dict(pipeline_mode=pl.Buffered(1))
    full = lambda shape: pl.BlockSpec(shape, whole, **one)
    out = pl.pallas_call(
        functools.partial(mlp_kernel, steps=steps, chunk=chunk),
        grid_spec=pltpu.PrefetchScalarGridSpec(
            num_scalar_prefetch=1, grid=(steps,),
            in_specs=[full((toks, width)), full((toks, width)), full((toks, width)), full((width, width)), full((1, width)),
                      pl.BlockSpec((width, tile), lambda s, c: (0, s)),
                      pl.BlockSpec((width, tile), lambda s, c: (0, s + steps)),
                      pl.BlockSpec((tile, width), lambda s, c: (s, 0))],
            out_specs=[full((toks, width)), full((toks, width)), full((toks, width)), full((1, width)),
                       pl.BlockSpec((width, tile), lambda s, c: (0, s)), pl.BlockSpec((width, tile), lambda s, c: (0, s)),
                       pl.BlockSpec((tile, half), lambda s, c: (s, 0)), pl.BlockSpec((tile, half), lambda s, c: (s, 0)),
                       full((width, half)), full((width, half))],
            scratch_shapes=[pltpu.VMEM((toks, width), F32)] * 3 + [pltpu.VMEM((toks, width), BF), pltpu.VMEM((width, toks), BF)]
                         + [pltpu.VMEM((toks, tile), BF)] * 3),
        out_shape=[jax.ShapeDtypeStruct((toks, width), BF), jax.ShapeDtypeStruct((toks, width), F32), jax.ShapeDtypeStruct((toks, width), BF),
                   jax.ShapeDtypeStruct((1, width), F32),
                   jax.ShapeDtypeStruct((width, ff), BF), jax.ShapeDtypeStruct((width, ff), BF),
                   jax.ShapeDtypeStruct((ff, half), BF), jax.ShapeDtypeStruct((ff, half), BF),
                   jax.ShapeDtypeStruct((width, half), BF), jax.ShapeDtypeStruct((width, half), BF)],
        compiler_params=pltpu.CompilerParams(vmem_limit_bytes=60 * MIB, dimension_semantics=("arbitrary",)),
        cost_estimate=pl.CostEstimate(flops=2 * toks * width * (9 * ff + 3 * width), bytes_accessed=60 * MIB, transcendentals=toks * ff),
        name="mlp",
    )(core, mixed, tokens, cot, w_out, gain.reshape(1, width), w_gate_up, w_gate_up, w_down)
    return out

HEADS=16; FEAT=16; WINDOW=64; ROWS_PHI=160

def lane_mask(width, size, which, dtype=BF):
    lanes = lax.broadcasted_iota(jnp.int32, (1, width), 1)
    return (lanes // size == which).astype(dtype)

def features_t(x):
    feat, toks = x.shape
    both = jnp.concatenate([x, x], axis=0)
    parts = [x * x * (2.0 * feat) ** -0.5]
    xs = x * feat ** -0.5
    for d in range(1, feat // 2):
        parts.append(xs * both[d:d + feat])
    parts.append(x * feat ** -0.25)
    parts.append(xs[:feat // 2] * x[feat // 2:])
    row = lax.broadcasted_iota(jnp.int32, (8, toks), 0)
    parts.append((row == 0).astype(F32))
    return jnp.concatenate(parts, axis=0)

def features_back_t(x, g):
    feat, toks = x.shape
    half = feat // 2
    both = jnp.concatenate([x, x], axis=0)
    total = g[:feat] * x * (2.0 * (2.0 * feat) ** -0.5)
    mixed = jnp.zeros((feat, toks), F32)
    for d in range(1, half):
        gd = g[d * feat:(d + 1) * feat]
        mixed = mixed + gd * both[d:d + feat]
        gx = gd * x
        mixed = mixed + jnp.concatenate([gx[feat - d:], gx[:feat - d]], axis=0)
    g8 = g[(half + 1) * feat:(half + 1) * feat + half]
    mixed = mixed + jnp.concatenate([g8 * x[half:], g8 * x[:half]], axis=0)
    return total + mixed * feat ** -0.5 + g[half * feat:(half + 1) * feat] * feat ** -0.25

def states_of(x_t, y, group):
    out = None
    size = y.shape[1] // 4
    for h in range(4):
        x = x_t[pl.ds(pl.multiple_of(group * 4 * FEAT + h * FEAT, FEAT), FEAT), :]
        s = nn(features_t(x).astype(BF), y * lane_mask(4 * size, size, h))
        out = s if out is None else out + s
    return out

def state_kernel(k, v, owned, out, k_t):
    g = pl.program_id(1)
    @pl.when(g == 0)
    def _():
        k_t[...] = k[...].astype(F32).T
    out[0, 0] = states_of(k_t, v[...] * owned[...].astype(BF), g)

def spec_tok(rows_len, width):
    return pl.BlockSpec((rows_len, width), lambda r, g: (r, g))
def spec_col(rows_len, first):
    return pl.BlockSpec((rows_len, 256), lambda r, g: (r, first + g))
def spec_all(rows_len, width):
    return pl.BlockSpec((rows_len, width), lambda r, g: (r, 0))
SPEC_STATE = pl.BlockSpec((1, 1, ROWS_PHI, 256), lambda r, g: (r, g, 0, 0))
PARAMS = pltpu.CompilerParams(vmem_limit_bytes=56 * MIB, dimension_semantics=("arbitrary", "arbitrary"))

def local_states(first, owned, rows, length):
    groups = HEADS // 4
    return pl.pallas_call(
        state_kernel, grid=(rows, groups),
        in_specs=[spec_all(length, 256), spec_col(length, 1), spec_all(length, 1)],
        out_specs=SPEC_STATE,
        out_shape=jax.ShapeDtypeStruct((rows, groups, ROWS_PHI, 256), F32),
        scratch_shapes=[pltpu.VMEM((256, length), F32)],
        compiler_params=PARAMS, name="state",
        cost_estimate=pl.CostEstimate(flops=rows*groups*4*2*ROWS_PHI*256*length, bytes_accessed=6*MIB, transcendentals=0),
    )(first, first, owned)

def intra_kernel(q, k, v, low, end, out, mask, *, length):
    g = pl.program_id(1)
    half = length // 2
    @pl.when(g == 0)
    def _():
        i = lax.broadcasted_iota(jnp.int32, (length, length), 0)
        j = lax.broadcasted_iota(jnp.int32, (length, length), 1)
        mask[...] = ((j >= low[...]) & (j <= i) & (j < end[...])).astype(BF)
    qv, kv, vv = q[...], k[...], v[...]
    top = bottom = None
    for h in range(4):
        km = kv * lane_mask(HEADS * FEAT, FEAT, g * 4 + h)
        vm = vv * lane_mask(256, 64, h)
        u0 = 1.0 + nt(qv[:half], km[:half]) * FEAT ** -0.5
        a0 = (0.5 + 0.5 * u0 * u0).astype(BF) * mask[:half, :half]
        u1 = 1.0 + nt(qv[half:], km) * FEAT ** -0.5
        a1 = (0.5 + 0.5 * u1 * u1).astype(BF) * mask[half:, :]
        o0, o1 = nn(a0, vm[:half]), nn(a1, vm)
        top = o0 if top is None else top + o0
        bottom = o1 if bottom is None else bottom + o1
    out[:half, :] = top
    out[half:, :] = bottom

def intra(first, second, low, end, rows, length):
    groups = HEADS // 4
    return pl.pallas_call(
        functools.partial(intra_kernel, length=length), grid=(rows, groups),
        in_specs=[spec_all(length, 256), spec_all(length, 256), spec_col(length, 1), spec_all(length, 1), spec_all(length, 1)],
        out_specs=spec_tok(length, 256),
        out_shape=jax.ShapeDtypeStruct((rows * length, 1024), F32),
        scratch_shapes=[pltpu.VMEM((length, length), BF)],
        compiler_params=PARAMS, name="intra",
        cost_estimate=pl.CostEstimate(flops=rows*HEADS*2*6*256*256*256, bytes_accessed=8*MIB, transcendentals=0),
    )(second, first, first, low, end)

def window_mask_t(low, high):
    key = lax.broadcasted_iota(jnp.int32, (2 * WINDOW, 4 * WINDOW), 0)
    query = lax.broadcasted_iota(jnp.int32, (2 * WINDOW, 4 * WINDOW), 1) % WINDOW
    return (key >= query) & (key <= query + WINDOW) & (key >= low) & (key < high)

def stacked(x):
    return jnp.concatenate([x * lane_mask(256, 64, h) for h in range(4)], axis=0)

def unstacked(x):
    total = None
    for h in range(4):
        part = x[h * WINDOW:(h + 1) * WINDOW] * lane_mask(256, 64, h, F32)
        total = part if total is None else total + part
    return total

def window_kernel(low, high, q, k, v, hk, hv, out, ka, va, *, length, per_row):
    r = pl.program_id(0)
    ka[:WINDOW, :] = hk[...]
    ka[WINDOW:, :] = k[...]
    va[:WINDOW, :] = hv[...]
    va[WINDOW:, :] = v[...]
    for n in range(length // WINDOW):
        keys = ka[n * WINDOW:(n + 2) * WINDOW, :]
        vals = va[n * WINDOW:(n + 2) * WINDOW, :]
        s = nt(stacked(q[n * WINDOW:(n + 1) * WINDOW, :]), keys) * 64 ** -0.5
        key = lax.broadcasted_iota(jnp.int32, (4 * WINDOW, 2 * WINDOW), 1)
        query = lax.broadcasted_iota(jnp.int32, (4 * WINDOW, 2 * WINDOW), 0) % WINDOW
        ok = (key >= query) & (key <= query + WINDOW) & (key >= low[r * per_row + n]) & (key < high[r * per_row + n])
        s = jnp.where(ok, s, -1e30)
        p = jnp.exp(s - jnp.max(s, axis=1, keepdims=True))
        p = (p / jnp.sum(p, axis=1, keepdims=True)).astype(BF)
        out[n * WINDOW:(n + 1) * WINDOW, :] = unstacked(nn(p, vals))

def smem_spec():
    return pl.BlockSpec(memory_space=pltpu.SMEM)

def window(low, high, first, second, hk, hv, rows, length):
    groups = HEADS // 4
    return pl.pallas_call(
        functools.partial(window_kernel, length=length, per_row=length // WINDOW), grid=(rows, groups),
        in_specs=[smem_spec(), smem_spec(), spec_col(length, 1), spec_col(length, 5), spec_col(length, 1), spec_tok(WINDOW, 256), spec_tok(WINDOW, 256)],
        out_specs=spec_tok(length, 256),
        out_shape=jax.ShapeDtypeStruct((rows * length, 1024), F32),
        scratch_shapes=[pltpu.VMEM((length + WINDOW, 256), BF)] * 2,
        compiler_params=PARAMS, name="window",
        cost_estimate=pl.CostEstimate(flops=rows*HEADS*2*4*length*128*256, bytes_accessed=8*MIB, transcendentals=0),
    )(low, high, second, second, first, hk, hv)

def window_back_kernel(low, high, q, k, v, hk, hv, go, dq, dk, dv, dhk, dhv, ka, va, dka, dva, *, length, per_row):
    r = pl.program_id(0)
    ka[:WINDOW, :] = hk[...]
    ka[WINDOW:, :] = k[...]
    va[:WINDOW, :] = hv[...]
    va[WINDOW:, :] = v[...]
    carry_k = carry_v = None
    for n in range(length // WINDOW):
        keys = ka[n * WINDOW:(n + 2) * WINDOW, :]
        vals = va[n * WINDOW:(n + 2) * WINDOW, :]
        qs = stacked(q[n * WINDOW:(n + 1) * WINDOW, :])
        gs = stacked(go[n * WINDOW:(n + 1) * WINDOW, :])
        s = nt(keys, qs) * 64 ** -0.5
        s = jnp.where(window_mask_t(low[r * per_row + n], high[r * per_row + n]), s, -1e30)
        p = jnp.exp(s - jnp.max(s, axis=0, keepdims=True))
        p = p * (1.0 / jnp.sum(p, axis=0, keepdims=True))
        gp = nt(vals, gs)
        ds = (p * (gp - jnp.sum(p * gp, axis=0, keepdims=True)) * 64 ** -0.5).astype(BF)
        dk_n = nn(ds, qs)
        dv_n = nn(p.astype(BF), gs)
        dq[n * WINDOW:(n + 1) * WINDOW, :] = unstacked(tn(ds, keys)).astype(BF)
        if n == 0:
            dhk[...] = dk_n[:WINDOW].astype(BF)
            dhv[...] = dv_n[:WINDOW].astype(BF)
        else:
            dk[(n - 1) * WINDOW:n * WINDOW, :] = (carry_k + dk_n[:WINDOW]).astype(dk.dtype)
            dv[(n - 1) * WINDOW:n * WINDOW, :] = carry_v + dv_n[:WINDOW]
        carry_k, carry_v = dk_n[WINDOW:], dv_n[WINDOW:]
    dk[length - WINDOW:, :] = carry_k.astype(dk.dtype)
    dv[length - WINDOW:, :] = carry_v

def window_back(low, high, first, second, hk, hv, go, rows, length):
    groups = HEADS // 4
    total = rows * length
    return pl.pallas_call(
        functools.partial(window_back_kernel, length=length, per_row=length // WINDOW), grid=(rows, groups),
        in_specs=[smem_spec(), smem_spec(), spec_col(length, 1), spec_col(length, 5), spec_col(length, 1), spec_tok(WINDOW, 256), spec_tok(WINDOW, 256), spec_tok(length, 256)],
        out_specs=[spec_tok(length, 256)] * 3 + [spec_tok(WINDOW, 256)] * 2,
        out_shape=[jax.ShapeDtypeStruct((total, 1024), BF), jax.ShapeDtypeStruct((total, 1024), F32), jax.ShapeDtypeStruct((total, 1024), F32),
                   jax.ShapeDtypeStruct((rows * WINDOW, 1024), BF), jax.ShapeDtypeStruct((rows * WINDOW, 1024), BF)],
        scratch_shapes=[pltpu.VMEM((length + WINDOW, 256), BF)] * 2 + [pltpu.VMEM((8, 256), F32)] * 2,
        compiler_params=PARAMS, name="window_back",
        cost_estimate=pl.CostEstimate(flops=rows*HEADS*2*10*length*128*256, bytes_accessed=16*MIB, transcendentals=0),
    )(low, high, second, second, first, hk, hv, go)

def piece_mean(x):
    a = lax.broadcasted_iota(jnp.int32, (256, 256), 0) // 64
    b = lax.broadcasted_iota(jnp.int32, (256, 256), 1) // 64
    ones = jnp.where(a == b, 1.0 / 64, 0.0).astype(BF)
    high = x.astype(BF)
    return nn(high, ones) + nn((x - high.astype(F32)).astype(BF), ones)

def through_state(x_t, state, group):
    state_t = state.T.astype(BF)
    parts = []
    for h in range(4):
        x = x_t[pl.ds(pl.multiple_of(group * 4 * FEAT + h * FEAT, FEAT), FEAT), :]
        parts.append(nn(state_t[h * 64:(h + 1) * 64], features_t(x).astype(BF)))
    return jnp.concatenate(parts, axis=0).T

def mix_kernel(q, state, local, windowed, early, numer, mixed, q_t):
    g = pl.program_id(1)
    @pl.when(g == 0)
    def _():
        q_t[...] = q[...].astype(F32).T
    num = local[...] + through_state(q_t, state[0, 0].astype(F32), g) * early[...]
    rho = lax.rsqrt(piece_mean(num * num) + EPSILON)
    numer[...] = num
    mixed[...] = (num * rho + windowed[...]).astype(BF)

def mix(q, state, local, windowed, early, rows, length):
    groups = HEADS // 4
    total = rows * length
    return pl.pallas_call(
        mix_kernel, grid=(rows, groups),
        in_specs=[spec_all(length, 256), SPEC_STATE, spec_tok(length, 256), spec_tok(length, 256), spec_all(length, 1)],
        out_specs=[spec_tok(length, 256)] * 2,
        out_shape=[jax.ShapeDtypeStruct((total, 1024), F32), jax.ShapeDtypeStruct((total, 1024), BF)],
        scratch_shapes=[pltpu.VMEM((256, length), F32)],
        compiler_params=PARAMS, name="mix",
        cost_estimate=pl.CostEstimate(flops=rows*HEADS*2*1024*256*256, bytes_accessed=18*MIB, transcendentals=0),
    )(q, state, local, windowed, early)

def numer_back_kernel(q, numer, gm, early, grad_numer, grad_state, q_t):
    g = pl.program_id(1)
    @pl.when(g == 0)
    def _():
        q_t[...] = q[...].astype(F32).T
    num = numer[...]
    rho = lax.rsqrt(piece_mean(num * num) + EPSILON)
    lin = num * rho
    gl = gm[...].astype(F32)
    gn = (rho * (gl - lin * piece_mean(gl * lin))).astype(BF)
    grad_numer[...] = gn
    grad_state[0, 0] = states_of(q_t, gn * early[...].astype(BF), g)

def numer_back(q, numer, gm, early, rows, length):
    groups = HEADS // 4
    total = rows * length
    return pl.pallas_call(
        numer_back_kernel, grid=(rows, groups),
        in_specs=[spec_all(length, 256), spec_tok(length, 256), spec_tok(length, 256), spec_all(length, 1)],
        out_specs=[spec_tok(length, 256), SPEC_STATE],
        out_shape=[jax.ShapeDtypeStruct((total, 1024), BF), jax.ShapeDtypeStruct((rows, groups, ROWS_PHI, 256), F32)],
        scratch_shapes=[pltpu.VMEM((256, length), F32)],
        compiler_params=PARAMS, name="numer_back",
        cost_estimate=pl.CostEstimate(flops=rows*HEADS*2*1024*256*256, bytes_accessed=10*MIB, transcendentals=0),
    )(q, numer, gm, early)

def intra_back_kernel(q, k, v, gn, dv_in, low, end, early_r, state, dq, dk_t, dv, mask, q_t, k_t, dq_t, *, length):
    g = pl.program_id(1)
    half = length // 2
    @pl.when(g == 0)
    def _():
        j = lax.broadcasted_iota(jnp.int32, (length, length), 0)
        i = lax.broadcasted_iota(jnp.int32, (length, length), 1)
        mask[...] = ((j >= low[0]) & (j <= i) & (j < end[0])).astype(BF)
        q_t[...] = q[...].astype(F32).T
        k_t[...] = k[...].astype(F32).T
    qv, kv, vv, gv = q[...], k[...], v[...], gn[...]
    st = state[0, 0].astype(BF)
    top = dv_in[:half, :]
    bottom = dv_in[half:, :]
    for h in range(4):
        at = pl.ds(pl.multiple_of(g * 4 * FEAT + h * FEAT, FEAT), FEAT)
        km = kv * lane_mask(HEADS * FEAT, FEAT, g * 4 + h)
        vm = vv * lane_mask(256, 64, h)
        gm = gv * lane_mask(256, 64, h)
        qx, kx = q_t[at, :], k_t[at, :]
        qb, kb = qx.astype(BF), kx.astype(BF)
        u0 = 1.0 + nt(km[:half], qv) * FEAT ** -0.5
        u1 = 1.0 + nt(km[half:], qv[half:]) * FEAT ** -0.5
        ga0 = nt(vm[:half], gv)
        ga1 = nt(vm[half:], gv[half:])
        m0, m1 = mask[:half, :], mask[half:, half:]
        a0 = (0.5 + 0.5 * u0 * u0).astype(BF) * m0
        a1 = (0.5 + 0.5 * u1 * u1).astype(BF) * m1
        ds0 = (ga0 * u0 * FEAT ** -0.5).astype(BF) * m0
        ds1 = (ga1 * u1 * FEAT ** -0.5).astype(BF) * m1
        top = top + nn(a0, gm)
        bottom = bottom + nn(a1, gm[half:])
        dk_t[0, at, :half] = nt(qb, ds0)
        dk_t[0, at, half:] = nt(qb[:, half:], ds1)
        d = nn(kb[:, :half], ds0)
        d = d + jnp.concatenate([jnp.zeros((FEAT, half), F32), nn(kb[:, half:], ds1)], axis=1)
        gphi = nt(st * lane_mask(256, 64, h), gv) * early_r[0]
        dq_t[at, :] = d + features_back_t(qx, gphi)
    dv[:half, :] = top
    dv[half:, :] = bottom
    @pl.when(g == pl.num_programs(1) - 1)
    def _():
        dq[...] = dq_t[...].T.astype(BF)

def intra_back(first, second, gn, dv_in, low, end, early_r, state, rows, length):
    groups = HEADS // 4
    total = rows * length
    return pl.pallas_call(
        functools.partial(intra_back_kernel, length=length), grid=(rows, groups),
        in_specs=[spec_all(length, 256), spec_all(length, 256), spec_col(length, 1), spec_tok(length, 256), spec_tok(length, 256),
                  pl.BlockSpec((1, 1, length), lambda r, g: (r, 0, 0)),
                  pl.BlockSpec((1, 1, length), lambda r, g: (r, 0, 0)), pl.BlockSpec((1, 1, length), lambda r, g: (r, 0, 0)), SPEC_STATE],
        out_specs=[spec_all(length, 256), pl.BlockSpec((1, 256, length), lambda r, g: (r, 0, 0)), spec_tok(length, 256)],
        out_shape=[jax.ShapeDtypeStruct((total, 256), BF), jax.ShapeDtypeStruct((rows, 256, length), F32), jax.ShapeDtypeStruct((total, 1024), F32)],
        scratch_shapes=[pltpu.VMEM((length, length), BF)] + [pltpu.VMEM((256, length), F32)] * 3,
        compiler_params=PARAMS, name="intra_back",
        cost_estimate=pl.CostEstimate(flops=rows*HEADS*2*15*256*256*256, bytes_accessed=14*MIB, transcendentals=0),
    )(second, first, first, gn, dv_in, low, end, early_r, state)

def state_back_kernel(k, v, dk_in, dv_in, dhv, owned_r, owned_c, state, dk, dv, k_t, dk_t, *, length):
    g = pl.program_id(1)
    @pl.when(g == 0)
    def _():
        k_t[...] = k[...].astype(F32).T
    st = state[0, 0].astype(F32)
    sb = st.astype(BF)
    vv = v[...]
    dvs = through_state(k_t, st, g) * owned_c[...]
    tail = length - WINDOW
    dv[:tail, :] = (dv_in[:tail, :] + dvs[:tail]).astype(BF)
    dv[tail:, :] = (dv_in[tail:, :] + dvs[tail:] + dhv[...].astype(F32)).astype(BF)
    for h in range(4):
        at = pl.ds(pl.multiple_of(g * 4 * FEAT + h * FEAT, FEAT), FEAT)
        gphi = nt(sb * lane_mask(256, 64, h), vv) * owned_r[0]
        dk_t[at, :] = dk_in[0, at, :] + features_back_t(k_t[at, :], gphi)
    @pl.when(g == pl.num_programs(1) - 1)
    def _():
        dk[...] = dk_t[...].T.astype(BF)

def state_back(first, dk_in, dv_in, dhv, owned_r, owned_c, state, rows, length):
    groups = HEADS // 4
    total = rows * length
    return pl.pallas_call(
        functools.partial(state_back_kernel, length=length), grid=(rows, groups),
        in_specs=[spec_all(length, 256), spec_col(length, 1), pl.BlockSpec((1, 256, length), lambda r, g: (r, 0, 0)), spec_tok(length, 256),
                  spec_tok(WINDOW, 256), pl.BlockSpec((1, 1, length), lambda r, g: (r, 0, 0)), spec_all(length, 1), SPEC_STATE],
        out_specs=[spec_all(length, 256), spec_tok(length, 256)],
        out_shape=[jax.ShapeDtypeStruct((total, 256), BF), jax.ShapeDtypeStruct((total, 1024), BF)],
        scratch_shapes=[pltpu.VMEM((256, length), F32)] * 2,
        compiler_params=PARAMS, name="state_back",
        cost_estimate=pl.CostEstimate(flops=rows*HEADS*2*1024*256*256, bytes_accessed=14*MIB, transcendentals=0),
    )(first, first, dk_in, dv_in, dhv, owned_r, owned_c, state)


def proj_kernel(tokens, gain, w, normed, out):
    @pl.when(pl.program_id(0) == 0)
    def _():
        x = tokens[...].astype(F32)
        normed[...] = (x * lax.rsqrt(jnp.mean(x * x, axis=-1, keepdims=True) + EPSILON) * gain[...]).astype(BF)
    out[...] = nn(normed[...], w[...]).astype(BF)

def proj_more_kernel(normed, w, out):
    out[...] = nn(normed[...], w[...]).astype(BF)

def project(tokens, gain, w_in):
    toks, width = tokens.shape
    tiles = w_in.shape[1] // 256
    lin = HEADS * FEAT // 256
    heads = width // 256
    whole = lambda s: (0, 0)
    one = dict(pipeline_mode=pl.Buffered(1))
    params = pltpu.CompilerParams(vmem_limit_bytes=56 * MIB, dimension_semantics=("arbitrary",))
    count = 1 + heads
    normed, first = pl.pallas_call(
        proj_kernel, grid=(count,),
        in_specs=[pl.BlockSpec((toks, width), whole, **one), pl.BlockSpec((1, width), whole),
                  pl.BlockSpec((width, 256), lambda s: (0, jnp.where(s == 0, 1, tiles - count + s)))],
        out_specs=[pl.BlockSpec((toks, width), whole, **one), pl.BlockSpec((toks, 256), lambda s: (0, s))],
        out_shape=[jax.ShapeDtypeStruct((toks, width), BF), jax.ShapeDtypeStruct((toks, 256 * count), BF)],
        compiler_params=params, name="project_keys",
        cost_estimate=pl.CostEstimate(flops=2 * toks * width * 256 * count, bytes_accessed=10 * MIB, transcendentals=0),
    )(tokens, gain.reshape(1, width), w_in)
    rest = tiles - count
    second = pl.pallas_call(
        proj_more_kernel, grid=(rest,),
        in_specs=[pl.BlockSpec((toks, width), whole, **one), pl.BlockSpec((width, 256), lambda s: (0, jnp.where(s == 0, 0, s + 1)))],
        out_specs=pl.BlockSpec((toks, 256), lambda s: (0, s)),
        out_shape=jax.ShapeDtypeStruct((toks, 256 * rest), BF),
        compiler_params=params, name="project_rest",
        cost_estimate=pl.CostEstimate(flops=2 * toks * width * 256 * rest, bytes_accessed=12 * MIB, transcendentals=0),
    )(normed, w_in)
    return normed, first, second

def swap(x, bit, count):
    return lax.ppermute(x, "seq", [(i, i ^ (1 << bit)) for i in range(count)])

def pick(x, index, axis):
    return lax.dynamic_index_in_dim(x, index, axis, False)

def scan_states(local, table, me, count, backward):
    bits = count.bit_length() - 1
    core = me % 2
    flags = pick(table, core, 1)
    place = jnp.arange(count, dtype=jnp.int32)
    chip = me - core
    order = jnp.arange(1, bits, dtype=jnp.int32)
    base = (me >> (order + 1)) << (order + 1)
    middle = base + (1 << order)
    upper = ((me >> order) & 1) == 1
    def flagged(low, high):
        inside = (place[None, :] >= low[:, None]) & (place[None, :] < high[:, None])
        return jnp.max(jnp.where(inside, flags[None, :], 0.0), axis=1)
    if backward:
        cut = 1.0 - flagged(base, middle)
        stop = 1.0 - flagged(jnp.full_like(base, chip + 2), middle)
        own, other = jnp.where(upper, cut, 1.0), jnp.where(upper, 1.0, cut)
        into = jnp.where(upper, 0.0, stop)
    else:
        cut = 1.0 - flagged(middle, base + (2 << order))
        stop = 1.0 - flagged(middle, jnp.full_like(base, chip))
        own, other = jnp.where(upper, 1.0, cut), jnp.where(upper, cut, 1.0)
        into = jnp.where(upper, stop, 0.0)
    f0 = pick(flags, chip, 0)
    f1 = pick(flags, chip + 1, 0)
    mine = pick(local, core, 0)
    theirs = swap(pick(local, 1 - core, 0).astype(BF), 0, count).astype(F32)
    at0 = jnp.where(core == 0, mine, theirs)
    at1 = jnp.where(core == 0, theirs, mine)
    total = (at0 + (1.0 - f0) * at1 if backward else at1 + (1.0 - f1) * at0).astype(BF)
    entering = jnp.zeros_like(mine)
    for b in range(1, bits):
        received = swap(total, b, count).astype(F32)
        entering = entering + into[b - 1] * received
        if b < bits - 1:
            total = (own[b - 1] * total.astype(F32) + other[b - 1] * received).astype(BF)
    if backward:
        x1, x0 = entering, at1 + (1.0 - f1) * entering
    else:
        x0, x1 = entering, at0 + (1.0 - f0) * entering
    x0, x1 = x0.astype(BF), x1.astype(BF)
    keep = jnp.where(core == 0, x0, x1)
    back = swap(jnp.where(core == 0, x1, x0), 0, count)
    return jnp.stack([jnp.where(core == 0, keep, back), jnp.where(core == 0, back, keep)])

def halve(keep, received, me, count, order):
    left = list(range(count.bit_length() - 2, 0, -1))
    for b in order:
        at = left.index(b)
        left.remove(b)
        mine = (me >> b) & 1
        def part(x, which):
            x = x.reshape((1 << at, 2, -1) + x.shape[1:])
            x = pick(x, which, 1)
            return x.reshape((-1,) + x.shape[2:])
        send = part(keep, 1 - mine) + part(received, 1 - mine)
        keep = part(keep, mine) + part(received, mine)
        received = swap(send, b, count)
    return keep[0].astype(F32) + received[0].astype(F32)

def finish(rows, me, count):
    core = me % 2
    each = rows.shape[0] // 2
    own = lax.dynamic_slice_in_dim(rows, core * each, each, 0)
    got = swap(lax.dynamic_slice_in_dim(rows, (1 - core) * each, each, 0), 0, count)
    return jnp.where(core == 0, own, got), jnp.where(core == 0, got, own)

def chips_first(x, chips):
    return x.reshape(chips, x.shape[0] // chips, x.shape[1])

def reduced(keep, send, me, count, order):
    chips = count // 2
    got = swap(send, 0, count)
    return finish(halve(chips_first(keep, chips), chips_first(got, chips), me, count, order), me, count)

def gain_sum(part, me):
    all_parts = lax.all_gather(part, "seq")
    each = part.shape[0] // all_parts.shape[0]
    return jnp.sum(lax.dynamic_slice_in_dim(all_parts, me * each, each, 1), axis=0)

def shards(tokens, seq_starts, seq_lengths, gain_in, gain_mlp, w_in, w_out, w_gate_up, w_down, cotangent):
    rows, length, width = tokens.shape
    count = lax.axis_size("seq")
    bits = count.bit_length() - 1
    order_a = list(range(1, bits))
    order_b = [2, 1] + list(range(3, bits))
    me = lax.axis_index("seq")
    core = me % 2
    total = rows * length
    begin = me * length
    ends = seq_starts + seq_lengths
    places = begin + jnp.arange(length, dtype=jnp.int32)
    last = seq_starts[:, -1:]
    reset = (last[:, 0] >= begin).astype(F32)
    early = (seq_starts < begin).astype(F32)
    owned = ((seq_starts == last) & (places[None, :] < ends)).astype(F32)
    low, end = seq_starts - begin, ends - begin
    column = lambda x: x.reshape(total, 1)
    line = lambda x: x.reshape(rows, 1, length)
    block_at = places[None, ::WINDOW] - WINDOW
    low_w = (seq_starts[:, ::WINDOW] - block_at).reshape(-1)
    high_w = (ends[:, ::WINDOW] - block_at).reshape(-1)
    table = lax.all_gather(reset, "seq")

    x = tokens.reshape(total, width)
    cot = cotangent.reshape(total, width)
    normed, first, second = project(x, gain_in, w_in)
    local_state = local_states(first, column(owned), rows, length)
    state_in = scan_states(local_state, table, me, count, False)

    tails = lambda a, at: a.reshape(rows, length, -1)[:, -WINDOW:, at:at + width]
    forward = [(i, i + 1) for i in range(count - 1)]
    backward = [(i + 1, i) for i in range(count - 1)]
    halo = lax.ppermute(jnp.stack([tails(second, 256 + width), tails(first, 256)]), "seq", forward)
    halo = halo.reshape(2, rows * WINDOW, width)
    local = intra(first, second, column(low), column(end), rows, length)
    windowed = window(low_w, high_w, first, second, halo[0], halo[1], rows, length)
    numer, mixed = mix(second, state_in, local, windowed, column(early), rows, length)
    (result, grad_resid, grad_mixed, gain_mlp_part, keep_gu, send_gu, keep_d, send_d, keep_o, send_o) = mlp(
        core.reshape(1), mixed, x, cot, w_out, gain_mlp, w_gate_up, w_down)
    part_gain_mlp = gain_sum(gain_mlp_part[0], me)
    grad_numer, grad_state_in = numer_back(second, numer, grad_mixed, column(early), rows, length)
    grad_state = scan_states(grad_state_in, table, me, count, True)
    part_gate_up = jnp.concatenate(reduced(keep_gu, send_gu, me, count, order_a), axis=1)
    part_down = jnp.concatenate(reduced(keep_d, send_d, me, count, order_b), axis=1)
    part_out = jnp.concatenate(reduced(keep_o, send_o, me, count, order_b), axis=1)

    dq_win, dk_win, dv_win, dhk, dhv = window_back(low_w, high_w, first, second, halo[0], halo[1], grad_mixed, rows, length)
    returned = lax.ppermute(jnp.stack([dhk, dhv]), "seq", backward).reshape(2, rows, WINDOW, width)
    dq_lin, dk_t, dv_part = intra_back(first, second, grad_numer, dv_win, line(low), line(end), line(early), state_in, rows, length)
    dk_lin, dv = state_back(first, dk_t, dv_part, returned[1].reshape(rows * WINDOW, width), line(owned), column(owned), grad_state, rows, length)
    dk_win = dk_win.reshape(rows, length, width)
    dk_win = jnp.concatenate([dk_win[:, :-WINDOW], dk_win[:, -WINDOW:] + returned[0].astype(F32)], axis=1).astype(BF).reshape(total, width)
    lin = HEADS * FEAT

    grad_projected = jnp.concatenate([dq_lin, dk_lin, dq_win, dk_win, dv], axis=1)
    grad_w = jnp.dot(normed.T, grad_projected, preferred_element_type=F32).astype(BF)
    half = grad_w.shape[1] // 2
    keep_i = lax.dynamic_slice_in_dim(grad_w, core * half, half, 1)
    send_i = lax.dynamic_slice_in_dim(grad_w, (1 - core) * half, half, 1)
    part_in = jnp.concatenate(reduced(keep_i, send_i, me, count, order_b), axis=1)
    grad_normed = jnp.dot(grad_projected, w_in.T, preferred_element_type=F32)
    stream = x.astype(F32)
    scale = lax.rsqrt(jnp.mean(stream * stream, axis=-1, keepdims=True) + EPSILON)
    part_gain_in = gain_sum(jnp.sum(grad_normed * stream * scale, axis=0), me)
    c = grad_normed * gain_in
    grad_tokens = grad_resid + scale * c - stream * (scale * scale * scale * jnp.mean(c * stream, axis=-1, keepdims=True))
    return (result.reshape(rows, length, width), grad_tokens.reshape(rows, length, width), part_gain_in, part_gain_mlp,
            part_in, part_out, part_gate_up, part_down)

def solution(mesh):
    split = P(None, "seq", None)
    placed = (split, P(None, "seq"), P(None, "seq"), P(), P(), P(), P(), P(), P(), split)
    return jax.shard_map(shards, mesh=mesh, in_specs=placed,
        out_specs=(split, split, P("seq"), P("seq"), P("seq", None), P("seq", None), P("seq", None), P("seq", None)),
        check_vma=False)
```

time: 1890 us -> 708 us (0.37)
  waiting for transfers between devices: 687 us -> 153 us
  matrix products: 467 us -> 25.6 us
  other arithmetic: 379 us -> 63.4 us
  Pallas kernels: 0 us -> 228 us
  local copies, waits for them, and re-layouts: 233 us -> 34.8 us
  blocking collectives: 86.9 us -> 163 us
  starting transfers between devices: 5.01 us -> 28 us
    all_gather x2 -> x0, waiting for transfers between devices: 486 us -> none  [entering(): lax.all_gather(a.astype(kind), axis)]
    dot_general x42 -> x2, matrix products: 467 us -> 25.6 us  [the longest x1 14.1 us: shards(): grad_normed = jnp.dot(grad_projected, w_in.T, preferred_element_type=F32)]
    pallas_call x0 -> x11, Pallas kernels: none -> 228 us  [the longest x1 88.9 us: mlp(): pl.pallas_call(functools.partial(mlp_kernel, steps=steps, chunk=chunk), g...]
    reduce_scatter x4 -> x0, waiting for transfers between devices: 201 us -> none  [the longest x1 170 us: shards(): lax.psum_scatter(grad_in_w, 'seq', scatter_dimension=0, tiled=True)]
    add x35 -> x25, other arithmetic: 177 us -> 24 us  [the longest x12 23.5 us: halve(): keep = part(keep, mine) + part(received, mine)]
    ppermute x2 -> x38, waiting for transfers between devices: 0.01 us -> 153 us  [the longest x36 153 us: swap(): return lax.ppermute(x, 'seq', [(i, i ^ 1 << bit) for i in range(count)])]
    dynamic_slice x62 -> x7, local copies, waits for them, and re-layouts: 136 us -> 4.34 us  [the longest x1 3.47 us: shards(): keep_i = lax.dynamic_slice_in_dim(grad_w, core * half, half, 1)]
    all_gather x0 -> x2, blocking collectives: none -> 118 us  [gain_sum(): all_parts = lax.all_gather(part, 'seq')]
  transfers between devices with their start and end apart: 8 -> 38, of which waited for: 4 -> 19; matrix products, arithmetic and copies ran while one was open for 46% -> 15% of each run, Pallas kernels for 0% -> 15%
where the time goes in v1:
time: 708 us; the launch traced here: 699 us
  Pallas kernels  228 us (32%)
  blocking collectives  163 us (23%)
  waiting for transfers between devices  153 us (22%)
  other arithmetic  63.4 us (9%)
  local copies, waits for them, and re-layouts  34.8 us (5%)
  starting transfers between devices  28 us (4%)
  matrix products  25.6 us (4%)
    ppermute x36, waiting for transfers between devices, swap(): return lax.ppermute(x, 'seq', [(i, i ^ 1 << bit) for i in range(count)])  153 us
    all_gather x2, blocking collectives, gain_sum(): all_parts = lax.all_gather(part, 'seq')  118 us
    pallas_call x1, Pallas kernels, mlp(): pl.pallas_call(functools.partial(mlp_kernel, steps=steps, chunk=chunk), g...  88.9 us
    unnamed x1, blocking collectives  44.4 us
    pallas_call x1, Pallas kernels, intra_back(): pl.pallas_call(functools.partial(intra_back_kernel, length=length), grid=...  26 us
    ppermute x36, starting transfers between devices, swap(): return lax.ppermute(x, 'seq', [(i, i ^ 1 << bit) for i in range(count)])  24.7 us
    pallas_call x1, Pallas kernels, window_back(): pl.pallas_call(functools.partial(window_back_kernel, length=length, per_r...  24.5 us
    add x12, other arithmetic, halve(): keep = part(keep, mine) + part(received, mine)  23.5 us
  transfers between devices with their start and end apart: 38, of which 19 were waited for; matrix products, arithmetic and copies ran while one was open for 15% of the time, Pallas kernels for 15%

profile of v1, /device:TPU:0, one launch (start us, length us, event | category | flops | bytes accessed | tf_op | source)
XLA Modules:
  0.0 698.6 jit_solution(18141768941487386051)
XLA Ops:
  4.1 8.1 %project_keys.1 = (bf16[1024,1024]{1,0:T(8,128)(2,1)}, bf16[1024,1280]{1,0:T(8,128)(2,1)}) custom-call(bf16[1024,1024]{1,0:T(8,128)(2,1)} %bitcast.236, f32[1,1024]{1,0:T(1,128)} %bitcast.284, bf16[1024,3584]{1,0:T(8,128)(2,1)} %w.3), custom_call_target="tpu_custom_call" | custom-call | flops 2684354560 | bytes 10485760 | tf_op jit(solution)/shard_map/project_keys/pallas_call | solution.py:516
  12.1 7.7 %state.1 = f32[2,4,160,256]{3,2,1,0:T(8,128)} custom-call(bf16[1024,1280]{1,0:T(8,128)(2,1)} %get-tuple-element.35.k.v, bf16[1024,1280]{1,0:T(8,128)(2,1)} %get-tuple-element.35.k.v, f32[1024,1]{1,0:T(8,128)} %bitcast.248), custom_call_target="tpu_custom_call" | custom-call | flops 1342177280 | bytes 6291456 | tf_op jit(solution)/shard_map/state/pallas_call | solution.py:201
  21.5 11.3 %project_rest.1.q.k = bf16[1024,2304]{1,0:T(8,128)(2,1)} custom-call(bf16[1024,1024]{1,0:T(8,128)(2,1)} %get-tuple-element.34.normed, bf16[1024,3584]{1,0:T(8,128)(2,1)} %w.3), custom_call_target="tpu_custom_call" | custom-call | flops 4831838208 | bytes 12582912 | tf_op jit(solution)/shard_map/project_rest/pallas_call | solution.py:526
  35.6 2.0 collective-permute-start.6
  38.1 44.4 %all-reduce = f32[64]{0:T(128)S(1)} all-reduce(f32[64]{0:T(128)S(1)} %dynamic-update-slice), channel_id=2, replica_groups=mesh['seq'=32] {'seq'}, use_global_device_ids=true, to_apply=%add | all-reduce | flops 64 | bytes 512
  84.4 2.3 collective-permute-start.1
  90.0 3.9 collective-permute-done.1
  93.9 1.4 fusion.11
  95.3 1.8 collective-permute-start.2
  97.1 13.3 %intra.1.local = f32[1024,1024]{1,0:T(8,128)} custom-call(bf16[1024,2304]{1,0:T(8,128)(2,1)} %project_rest.1.q.k, bf16[1024,1280]{1,0:T(8,128)(2,1)} %get-tuple-element.35.k.v, bf16[1024,1280]{1,0:T(8,128)(2,1)} %get-tuple-element.35.k.v, s32[1024,1]{1,0:T(8,128)} %bitcast.269, s32[1024,1]{1,0:T(8,128)} %bitcast.268), custom_call_target="tpu_custom_call" | custom-call | flops 6442450944 | bytes 8388608 | tf_op jit(solution)/shard_map/intra/pallas_call | solution.py:236
  110.7 1.3 fusion.13
  115.2 4.5 collective-permute-done.3
  119.7 1.3 fusion.15
  122.9 12.6 %collective-permute-done.4 = bf16[4,160,256]{2,1,0:T(8,128)(2,1)S(1)} collective-permute-done((bf16[4,160,256]{2,1,0:T(8,128)(2,1)S(1)}, bf16[4,160,256]{2,1,0:T(8,128)(2,1)S(1)}, u32[]{:S(2)}, u32[]{:S(2)}) %collective-permute-start.4) | collective-permute-done | bytes 327712 | tf_op jit(solution)/shard_map/ppermute | solution.py:537
  135.6 2.9 broadcast_select_fusion.2
  138.5 15.5 %window.1.windowed = f32[1024,1024]{1,0:T(8,128)} custom-call(s32[16]{0:T(128)} %reshape.624.low, s32[16]{0:T(128)} %reshape.625.high, bf16[1024,2304]{1,0:T(8,128)(2,1)} %project_rest.1.q.k, bf16[1024,2304]{1,0:T(8,128)(2,1)} %project_rest.1.q.k, bf16[1024,1280]{1,0:T(8,128)(2,1)} %get-tuple-element.35.k.v, bf16[128,1024]{1,0:T(8,128)(2,1)} %bitcast.255, ...), custom_call_target="tpu_custom_call" | custom-call | flops 4294967296 | bytes 8388608 | tf_op jit(solution)/shard_map/window/pallas_call | solution.py:284
  154.0 2.9 select_bitcast_fusion.3
  157.8 10.4 %mix.1 = (f32[1024,1024]{1,0:T(8,128)}, bf16[1024,1024]{1,0:T(8,128)(2,1)}) custom-call(bf16[1024,2304]{1,0:T(8,128)(2,1)} %project_rest.1.q.k, bf16[2,4,160,256]{3,2,1,0:T(8,128)(2,1)} %pad_maximum_fusion.2.state, f32[1024,1024]{1,0:T(8,128)} %intra.1.local, f32[1024,1024]{1,0:T(8,128)} %window.1.windowed, f32[1024,1]{1,0:T(8,128)} %bitcast.266), custom_call_target="tpu_custom_call" | custom-call | flops 4294967296 | bytes 18874368 | tf_op jit(solution)/shard_map/mix/pallas_call | solution.py:367
  168.2 88.9 %mlp.1 = (bf16[1024,1024]{1,0:T(8,128)(2,1)}, f32[1024,1024]{1,0:T(8,128)}, bf16[1024,1024]{1,0:T(8,128)(2,1)}, f32[1,1024]{1,0:T(1,128)}, bf16[1024,2816]{1,0:T...) custom-call(s32[1]{0:T(128)} %bitcast.core_ref, ...), custom_call_target="tpu_custom_call" | custom-call | flops 59592671232 | bytes 62914560 | tf_op jit(solution)/shard_map/mlp/pallas_call | solution.py:115
  257.1 11.3 %numer_back.1 = (bf16[1024,1024]{1,0:T(8,128)(2,1)}, f32[2,4,160,256]{3,2,1,0:T(8,128)}) custom-call(bf16[1024,2304]{1,0:T(8,128)(2,1)} %project_rest.1.q.k, f32[1024,1024]{1,0:T(8,128)} %get-tuple-element.39.numer, bf16[1024,1024]{1,0:T(8,128)(2,1)} %get-tuple-element.40.gm.go, f32[1024,1]{1,0:T(8,128)} %bitcast.267), custom_call_target="tpu_custom_call" | custom-call | flops 4294967296 | bytes 10485760 | tf_op jit(solution)/shard_map/numer_back/pallas_call | solution.py:393
  275.8 9.0 %collective-permute-done.9 = bf16[4,160,256]{2,1,0:T(8,128)(2,1)S(1)} collective-permute-done((bf16[4,160,256]{2,1,0:T(8,128)(2,1)S(1)}, bf16[4,160,256]{2,1,0:T(8,128)(2,1)S(1)}, u32[]{:S(2)}, u32[]{:S(2)}) %collective-permute-start.9) | collective-permute-done | bytes 327712 | tf_op jit(solution)/shard_map/ppermute | solution.py:537
  284.7 1.4 fusion.22
  287.1 24.5 %window_back.1 = (bf16[1024,1024]{1,0:T(8,128)(2,1)}, f32[1024,1024]{1,0:T(8,128)}, f32[1024,1024]{1,0:T(8,128)}, bf16[128,1024]{1,0:T(8,128)(2,1)}, bf16[128,1024]{1,0:T(8,128)(2,1)}) custom-call(s32[16]{0:T(128)} %reshape.624.low, s32[16]{0:T(128)} %reshape.625.high, bf16[1024,2304]{1,0:T(8,128)(2,1)} %project_rest.1.q.k, ...), custom_call_target="tpu_custom_call" | custom-call | flops 10737418240 | bytes 16777216 | tf_op jit(solution)/shard_map/window_back/pallas_call | solution.py:328
  315.4 3.2 collective-permute-start.11
  318.5 26.0 %intra_back.1 = (bf16[1024,256]{1,0:T(8,128)(2,1)}, f32[2,256,512]{2,1,0:T(8,128)}, f32[1024,1024]{1,0:T(8,128)}) custom-call(bf16[1024,2304]{1,0:T(8,128)(2,1)} %project_rest.1.q.k, bf16[1024,1280]{1,0:T(8,128)(2,1)} %get-tuple-element.35.k.v, bf16[1024,1280]{1,0:T(8,128)(2,1)} %get-tuple-element.35.k.v, bf16[1024,1024]{1,0:T(8,128)(2,1)} %get-tuple-element.41.gn, ...), custom_call_target="tpu_custom_call" | custom-call | flops 16106127360 | bytes 14680064 | tf_op jit(solution)/shard_map/intra_back/pallas_call | solution.py:450
  344.5 2.5 slice.152
  347.0 1.4 fusion.26
  350.1 14.0 %collective-permute-done.12 = bf16[4,160,256]{2,1,0:T(8,128)(2,1)S(1)} collective-permute-done((bf16[4,160,256]{2,1,0:T(8,128)(2,1)S(1)}, bf16[4,160,256]{2,1,0:T(8,128)(2,1)S(1)}, u32[]{:S(2)}, u32[]{:S(2)}) %collective-permute-start.12) | collective-permute-done | bytes 327712 | tf_op jit(solution)/shard_map/ppermute | solution.py:537
  364.1 2.9 broadcast_select_fusion
  368.6 2.9 select_bitcast_fusion.1
  372.5 11.3 %state_back.1 = (bf16[1024,256]{1,0:T(8,128)(2,1)}, bf16[1024,1024]{1,0:T(8,128)(2,1)}) custom-call(bf16[1024,1280]{1,0:T(8,128)(2,1)} %get-tuple-element.35.k.v, bf16[1024,1280]{1,0:T(8,128)(2,1)} %get-tuple-element.35.k.v, f32[2,256,512]{2,1,0:T(8,128)} %get-tuple-element.44.dk_in, f32[1024,1024]{1,0:T(8,128)} %get-tuple-element.45.dv_in, ...), custom_call_target="tpu_custom_call" | custom-call | flops 4294967296 | bytes 14680064 | tf_op jit(solution)/shard_map/state_back/pallas_call | solution.py:485
  383.8 1.9 constant_dynamic-update-slice_fusion.3
  385.7 1.5 constant_dynamic-update-slice_fusion.2
  387.3 1.6 constant_dynamic-update-slice_fusion.1
  389.6 1.5 constant_dynamic-update-slice_fusion
  391.2 11.5 %convolution_convert_fusion = bf16[1024,3584]{1,0:T(8,128)(2,1)S(1)} fusion(bf16[1024,1024]{1,0:T(8,128)(2,1)S(1)} %copy-done.14, bf16[1024,3584]{1,0:T(8,128)(2,1)} %constant_dynamic-update-slice_fusion), kind=kOutput, calls=%fused_computation | convolution fusion | flops 7519862784 | bytes 16777216 | tf_op jit(solution)/shard_map/dot_general | solution.py:678
  402.6 3.5 constant_dynamic-slice_fusion.1
  406.8 8.8 %collective-permute-done.20 = bf16[1024,512]{1,0:T(8,128)(2,1)S(1)} collective-permute-done((bf16[1024,512]{1,0:T(8,128)(2,1)}, bf16[1024,512]{1,0:T(8,128)(2,1)S(1)}, u32[]{:S(2)}, u32[]{:S(2)}) %collective-permute-start.20) | collective-permute-done | bytes 1048608 | tf_op jit(solution)/shard_map/ppermute | solution.py:537
  416.6 2.4 dynamic-slice_add_fusion.9
  420.2 13.0 %collective-permute-done.21 = bf16[8,64,512]{2,1,0:T(8,128)(2,1)S(1)} collective-permute-done((bf16[8,64,512]{2,1,0:T(8,128)(2,1)}, bf16[8,64,512]{2,1,0:T(8,128)(2,1)S(1)}, u32[]{:S(2)}, u32[]{:S(2)}) %collective-permute-start.21) | collective-permute-done | bytes 524320 | tf_op jit(solution)/shard_map/ppermute | solution.py:537
  435.7 6.0 collective-permute-done.22
  441.9 38.6 %all-gather.2 = f32[32,1,1024]{2,1,0:T(1,128)S(1)} all-gather(f32[1,1,1024]{2,1,0:T(1,128)S(1)} %bitcast.283), channel_id=1, replica_groups=mesh['seq'=32] {'seq'}, dimensions={0}, use_global_device_ids=true | all-gather | bytes 135168 | tf_op jit(solution)/shard_map/all_gather | solution.py:618
  481.2 4.7 dynamic-slice_add_fusion.3
  486.0 4.5 dynamic-slice_add_fusion.1
  490.5 2.0 collective-permute-start.15
  492.5 5.1 bitcast_add_fusion.1
  497.7 14.1 %fusion.3 = (f32[1024]{0:T(1024)S(1)}, f32[1024]{0:T(1024)S(1)}, f32[1024,1024]{1,0:T(8,128)}) fusion(f32[1024]{0:T(1024)S(1)} %bitcast.276, bf16[2,512,1024]{2,1,0:T(8,128)(2,1)S(1)} %copy-done.3, f32[1024]{0:T(1024)S(1)} %copy-done.13, bf16[1024,3584]{1,0:T(8,128)(2,1)} %constant_dynamic-update-slice_fusion, bf16[1024,3584]{1,0:T(8,128)(2,1)} %w.3), kind=kOutput, calls=%fused_computation.7 | convolution fusion | flops 7523530752 | bytes 20987904 | tf_op jit(solution)/shard_map/dot_general | solution.py:683
  511.9 79.6 %all-gather.1 = f32[32768]{0:T(1024)S(1)} all-gather(f32[1024]{0:T(1024)S(1)} %get-tuple-element.60), channel_id=3, replica_groups=mesh['seq'=32] {'seq'}, dimensions={0}, use_global_device_ids=true | all-gather | bytes 135168 | tf_op jit(solution)/shard_map/all_gather | solution.py:618
  592.1 1.9 dynamic-slice_add_fusion.6
  594.0 1.7 collective-permute-start.34
  595.7 6.4 fusion.1
  602.1 10.4 %collective-permute-done.34 = bf16[4,176,512]{2,1,0:T(8,128)(2,1)S(1)} collective-permute-done((bf16[4,176,512]{2,1,0:T(8,128)(2,1)S(1)}, bf16[4,176,512]{2,1,0:T(8,128)(2,1)S(1)}, u32[]{:S(2)}, u32[]{:S(2)}) %collective-permute-start.34) | collective-permute-done | bytes 720928 | tf_op jit(solution)/shard_map/ppermute | solution.py:537
  612.8 9.6 %collective-permute-done.35 = bf16[2,176,512]{2,1,0:T(8,128)(2,1)S(1)} collective-permute-done((bf16[2,176,512]{2,1,0:T(8,128)(2,1)S(1)}, bf16[2,176,512]{2,1,0:T(8,128)(2,1)S(1)}, u32[]{:S(2)}, u32[]{:S(2)}) %collective-permute-start.35) | collective-permute-done | bytes 360480 | tf_op jit(solution)/shard_map/ppermute | solution.py:537
  622.6 1.7 dynamic-slice_add_fusion.5
  624.2 1.7 collective-permute-start.16
  625.9 2.1 dynamic-slice_add_fusion.4
  628.8 3.6 collective-permute-done.36
  632.5 12.6 %collective-permute-done.16 = bf16[4,64,1792]{2,1,0:T(8,128)(2,1)S(1)} collective-permute-done((bf16[4,64,1792]{2,1,0:T(8,128)(2,1)S(1)}, bf16[4,64,1792]{2,1,0:T(8,128)(2,1)S(1)}, u32[]{:S(2)}, u32[]{:S(2)}) %collective-permute-start.16) | collective-permute-done | bytes 917536 | tf_op jit(solution)/shard_map/ppermute | solution.py:537
  646.0 9.4 %collective-permute-done.17 = bf16[2,64,1792]{2,1,0:T(8,128)(2,1)S(1)} collective-permute-done((bf16[2,64,1792]{2,1,0:T(8,128)(2,1)S(1)}, bf16[2,64,1792]{2,1,0:T(8,128)(2,1)S(1)}, u32[]{:S(2)}, u32[]{:S(2)}) %collective-permute-start.17) | collective-permute-done | bytes 458784 | tf_op jit(solution)/shard_map/ppermute | solution.py:537
  655.5 3.0 collective-permute-start.18
  658.5 1.4 collective-permute-done.28
  661.5 4.2 collective-permute-done.18
  665.9 12.7 %collective-permute-done.29 = bf16[2,64,2816]{2,1,0:T(8,128)(2,1)S(1)} collective-permute-done((bf16[2,64,2816]{2,1,0:T(8,128)(2,1)S(1)}, bf16[2,64,2816]{2,1,0:T(8,128)(2,1)S(1)}, u32[]{:S(2)}, u32[]{:S(2)}) %collective-permute-start.29) | collective-permute-done | bytes 720928 | tf_op jit(solution)/shard_map/ppermute | solution.py:537
  679.6 15.7 %collective-permute-done.30 = bf16[1,64,2816]{2,1,0:T(8,128)(2,1)S(1)} collective-permute-done((bf16[1,64,2816]{2,1,0:T(8,128)(2,1)S(1)}, bf16[1,64,2816]{2,1,0:T(8,128)(2,1)S(1)}, u32[]{:S(2)}, u32[]{:S(2)}) %collective-permute-start.30) | collective-permute-done | bytes 360480 | tf_op jit(solution)/shard_map/ppermute | solution.py:537
  (184 shorter events, 50.2 us)
Async XLA Ops:
  21.0 63.3 %collective-permute-start = (bf16[4,160,256]{2,1,0:T(8,128)(2,1)S(1)}, bf16[4,160,256]{2,1,0:T(8,128)(2,1)S(1)}, u32[]{:S(2)}, u32[]{:S(2)}) collective-permute-start(bf16[4,160,256]{2,1,0:T(8,128)(2,1)S(1)} %fusion.30), channel_id=1, source_target_pairs={{0,1},{1,0},{2,3},{3,2},{4,5},{5,4},{6,7},{7,6},{8,9},{9,8},{10,11... | collective-permute-start | bytes 983048 | tf_op jit(solution)/shard_map/ppermute | solution.py:537
  21.5 16.1 %copy-start.11 = (s32[2,512]{1,0:T(2,128)S(1)}, s32[2,512]{1,0:T(2,128)}, u32[]{:S(2)}) copy-start(s32[2,512]{1,0:T(2,128)} %param.11) | copy-start | bytes 12292
  21.5 62.8 %copy-start.1 = (f32[2,4,160,256]{3,2,1,0:T(8,128)S(1)}, f32[2,4,160,256]{3,2,1,0:T(8,128)}, u32[]{:S(2)}) copy-start(f32[2,4,160,256]{3,2,1,0:T(8,128)} %state.1) | copy-start | bytes 3932164
  35.6 86.5 %collective-permute-start.6 = (bf16[2,2,64,1024]{3,2,1,0:T(8,128)(2,1)}, bf16[2,2,64,1024]{3,2,1,0:T(8,128)(2,1)S(1)}, u32[]{:S(2)}, u32[]{:S(2)}) collective-permute-start(bf16[2,2,64,1024]{3,2,1,0:T(8,128)(2,1)} %pad_maximum_fusion.4), channel_id=1, source_target_pairs={{0,1},{1,2},{2,3},{3,4},{4,5},{5,6},{6,7},{7,8},{8,9},{9,10},{10,1... | collective-permute-start | bytes 1572872 | tf_op jit(solution)/shard_map/ppermute | solution.py:655
  84.4 9.5 %collective-permute-start.1 = (bf16[4,160,256]{2,1,0:T(8,128)(2,1)S(1)}, bf16[4,160,256]{2,1,0:T(8,128)(2,1)S(1)}, u32[]{:S(2)}, u32[]{:S(2)}) collective-permute-start(bf16[4,160,256]{2,1,0:T(8,128)(2,1)S(1)} %fusion.6), channel_id=1, source_target_pairs={{0,2},{1,3},{2,0},{3,1},{4,6},{5,7},{6,4},{7,5},{8,10},{9,11},{10,... | collective-permute-start | bytes 983048 | tf_op jit(solution)/shard_map/ppermute | solution.py:537
  95.3 15.4 %collective-permute-start.2 = (bf16[4,160,256]{2,1,0:T(8,128)(2,1)S(1)}, bf16[4,160,256]{2,1,0:T(8,128)(2,1)S(1)}, u32[]{:S(2)}, u32[]{:S(2)}) collective-permute-start(bf16[4,160,256]{2,1,0:T(8,128)(2,1)S(1)} %fusion.11), channel_id=1, source_target_pairs={{0,4},{1,5},{2,6},{3,7},{4,0},{5,1},{6,2},{7,3},{8,12},{9,13},{10,... | collective-permute-start | bytes 983048 | tf_op jit(solution)/shard_map/ppermute | solution.py:537
  112.0 7.7 %collective-permute-start.3 = (bf16[4,160,256]{2,1,0:T(8,128)(2,1)S(1)}, bf16[4,160,256]{2,1,0:T(8,128)(2,1)S(1)}, u32[]{:S(2)}, u32[]{:S(2)}) collective-permute-start(bf16[4,160,256]{2,1,0:T(8,128)(2,1)S(1)} %fusion.13), channel_id=1, source_target_pairs={{0,8},{1,9},{2,10},{3,11},{4,12},{5,13},{6,14},{7,15},{8,0},{9,1},... | collective-permute-start | bytes 983048 | tf_op jit(solution)/shard_map/ppermute | solution.py:537
  121.1 14.5 %collective-permute-start.4 = (bf16[4,160,256]{2,1,0:T(8,128)(2,1)S(1)}, bf16[4,160,256]{2,1,0:T(8,128)(2,1)S(1)}, u32[]{:S(2)}, u32[]{:S(2)}) collective-permute-start(bf16[4,160,256]{2,1,0:T(8,128)(2,1)S(1)} %fusion.15), channel_id=1, source_target_pairs={{0,16},{1,17},{2,18},{3,19},{4,20},{5,21},{6,22},{7,23},{8,24},{9,... | collective-permute-start | bytes 983048 | tf_op jit(solution)/shard_map/ppermute | solution.py:537
  138.4 15.6 %collective-permute-start.5 = (bf16[4,160,256]{2,1,0:T(8,128)(2,1)S(1)}, bf16[4,160,256]{2,1,0:T(8,128)(2,1)S(1)}, u32[]{:S(2)}, u32[]{:S(2)}) collective-permute-start(bf16[4,160,256]{2,1,0:T(8,128)(2,1)S(1)} %broadcast_select_fusion.2), channel_id=1, source_target_pairs={{0,1},{1,0},{2,3},{3,2},{4,5},{5,4},{6,7},{7,6},{8,9},{9,8},{10,11... | collective-permute-start | bytes 983048 | tf_op jit(solution)/shard_map/ppermute | solution.py:537
  269.6 4.2 collective-permute-start.8
  275.0 9.7 %collective-permute-start.9 = (bf16[4,160,256]{2,1,0:T(8,128)(2,1)S(1)}, bf16[4,160,256]{2,1,0:T(8,128)(2,1)S(1)}, u32[]{:S(2)}, u32[]{:S(2)}) collective-permute-start(bf16[4,160,256]{2,1,0:T(8,128)(2,1)S(1)} %fusion.17), channel_id=1, source_target_pairs={{0,2},{1,3},{2,0},{3,1},{4,6},{5,7},{6,4},{7,5},{8,10},{9,11},{10,... | collective-permute-start | bytes 983048 | tf_op jit(solution)/shard_map/ppermute | solution.py:537
  286.2 27.9 %collective-permute-start.10 = (bf16[4,160,256]{2,1,0:T(8,128)(2,1)S(1)}, bf16[4,160,256]{2,1,0:T(8,128)(2,1)S(1)}, u32[]{:S(2)}, u32[]{:S(2)}) collective-permute-start(bf16[4,160,256]{2,1,0:T(8,128)(2,1)S(1)} %fusion.22), channel_id=1, source_target_pairs={{0,4},{1,5},{2,6},{3,7},{4,0},{5,1},{6,2},{7,3},{8,12},{9,13},{10,... | collective-permute-start | bytes 983048 | tf_op jit(solution)/shard_map/ppermute | solution.py:537
  311.6 180.9 %collective-permute-start.26 = (bf16[1024,2816]{1,0:T(8,128)(2,1)}, bf16[1024,2816]{1,0:T(8,128)(2,1)}, u32[]{:S(2)}, u32[]{:S(2)}) collective-permute-start(bf16[1024,2816]{1,0:T(8,128)(2,1)} %get-tuple-element.57), channel_id=1, source_target_pairs={{0,1},{1,0},{2,3},{3,2},{4,5},{5,4},{6,7},{7,6},{8,9},{9,8},{10,11... | collective-permute-start | bytes 17301512 | tf_op jit(solution)/shard_map/ppermute | solution.py:537
  312.8 36.6 %collective-permute-start.7 = (bf16[2,128,1024]{2,1,0:T(8,128)(2,1)S(1)}, bf16[2,128,1024]{2,1,0:T(8,128)(2,1)S(1)}, u32[]{:S(2)}, u32[]{:S(2)}) collective-permute-start(bf16[2,128,1024]{2,1,0:T(8,128)(2,1)S(1)} %pad_maximum_fusion.5), channel_id=1, source_target_pairs={{1,0},{2,1},{3,2},{4,3},{5,4},{6,5},{7,6},{8,7},{9,8},{10,9},{11,1... | collective-permute-start | bytes 1572872 | tf_op jit(solution)/shard_map/ppermute | solution.py:670
  315.4 31.6 %collective-permute-start.11 = (bf16[4,160,256]{2,1,0:T(8,128)(2,1)S(1)}, bf16[4,160,256]{2,1,0:T(8,128)(2,1)S(1)}, u32[]{:S(2)}, u32[]{:S(2)}) collective-permute-start(bf16[4,160,256]{2,1,0:T(8,128)(2,1)S(1)} %fusion.24), channel_id=1, source_target_pairs={{0,8},{1,9},{2,10},{3,11},{4,12},{5,13},{6,14},{7,15},{8,0},{9,1},... | collective-permute-start | bytes 983048 | tf_op jit(solution)/shard_map/ppermute | solution.py:537
  344.5 3.9 copy-start.10
  344.5 19.5 %copy-start.6 = (f32[2,4,160,256]{3,2,1,0:T(8,128)S(1)}, f32[2,4,160,256]{3,2,1,0:T(8,128)}, u32[]{:S(2)}) copy-start(f32[2,4,160,256]{3,2,1,0:T(8,128)} %get-tuple-element.48) | copy-start | bytes 3932164
  348.4 15.7 %collective-permute-start.12 = (bf16[4,160,256]{2,1,0:T(8,128)(2,1)S(1)}, bf16[4,160,256]{2,1,0:T(8,128)(2,1)S(1)}, u32[]{:S(2)}, u32[]{:S(2)}) collective-permute-start(bf16[4,160,256]{2,1,0:T(8,128)(2,1)S(1)} %fusion.26), channel_id=1, source_target_pairs={{0,16},{1,17},{2,18},{3,19},{4,20},{5,21},{6,22},{7,23},{8,24},{9,... | collective-permute-start | bytes 983048 | tf_op jit(solution)/shard_map/ppermute | solution.py:537
  366.9 1.7 collective-permute-start.13
  372.5 13.2 %copy-start.7 = (bf16[1024,1024]{1,0:T(8,128)(2,1)S(1)}, bf16[1024,1024]{1,0:T(8,128)(2,1)}, u32[]{:S(2)}) copy-start(bf16[1024,1024]{1,0:T(8,128)(2,1)} %get-tuple-element.50) | copy-start | bytes 6291460
  387.3 2.3 copy-start.8
  388.9 2.3 copy-start.14
  406.1 29.1 %copy-start.2 = (bf16[2,512,1024]{2,1,0:T(8,128)(2,1)S(1)}, bf16[2,512,1024]{2,1,0:T(8,128)(2,1)}, u32[]{:S(2)}) copy-start(bf16[2,512,1024]{2,1,0:T(8,128)(2,1)} %param.10) | copy-start | bytes 6291460
  406.1 79.9 %collective-permute-start.14 = (bf16[1024,1792]{1,0:T(8,128)(2,1)}, bf16[1024,1792]{1,0:T(8,128)(2,1)}, u32[]{:S(2)}, u32[]{:S(2)}) collective-permute-start(bf16[1024,1792]{1,0:T(8,128)(2,1)} %get-tuple-element.77), channel_id=1, source_target_pairs={{0,1},{1,0},{2,3},{3,2},{4,5},{5,4},{6,7},{7,6},{8,9},{9,8},{10,11... | collective-permute-start | bytes 11010056 | tf_op jit(solution)/shard_map/ppermute | solution.py:537
  406.3 75.0 %collective-permute-start.32 = (bf16[2816,512]{1,0:T(8,128)(2,1)}, bf16[2816,512]{1,0:T(8,128)(2,1)}, u32[]{:S(2)}, u32[]{:S(2)}) collective-permute-start(bf16[2816,512]{1,0:T(8,128)(2,1)} %get-tuple-element.59), channel_id=1, source_target_pairs={{0,1},{1,0},{2,3},{3,2},{4,5},{5,4},{6,7},{7,6},{8,9},{9,8},{10,11... | collective-permute-start | bytes 8650760 | tf_op jit(solution)/shard_map/ppermute | solution.py:537
  406.6 9.0 %collective-permute-start.20 = (bf16[1024,512]{1,0:T(8,128)(2,1)}, bf16[1024,512]{1,0:T(8,128)(2,1)S(1)}, u32[]{:S(2)}, u32[]{:S(2)}) collective-permute-start(bf16[1024,512]{1,0:T(8,128)(2,1)} %get-tuple-element.55), channel_id=1, source_target_pairs={{0,1},{1,0},{2,3},{3,2},{4,5},{5,4},{6,7},{7,6},{8,9},{9,8},{10,11... | collective-permute-start | bytes 3145736 | tf_op jit(solution)/shard_map/ppermute | solution.py:537
  415.6 1.0 copy-start.9
  419.0 22.8 %copy-start.12 = (f32[1,1024]{1,0:T(1,128)S(1)}, f32[1,1024]{1,0:T(1,128)}, u32[]{:S(2)}) copy-start(f32[1,1024]{1,0:T(1,128)} %get-tuple-element.53) | copy-start | bytes 12292
  419.0 14.2 %collective-permute-start.21 = (bf16[8,64,512]{2,1,0:T(8,128)(2,1)}, bf16[8,64,512]{2,1,0:T(8,128)(2,1)S(1)}, u32[]{:S(2)}, u32[]{:S(2)}) collective-permute-start(bf16[8,64,512]{2,1,0:T(8,128)(2,1)} %bitcast.67), channel_id=1, source_target_pairs={{0,4},{1,5},{2,6},{3,7},{4,0},{5,1},{6,2},{7,3},{8,12},{9,13},{10,... | collective-permute-start | bytes 1572872 | tf_op jit(solution)/shard_map/ppermute | solution.py:537
  434.0 7.8 %collective-permute-start.22 = (bf16[4,64,512]{2,1,0:T(8,128)(2,1)}, bf16[4,64,512]{2,1,0:T(8,128)(2,1)S(1)}, u32[]{:S(2)}, u32[]{:S(2)}) collective-permute-start(bf16[4,64,512]{2,1,0:T(8,128)(2,1)} %get-tuple-element.93), channel_id=1, source_target_pairs={{0,2},{1,3},{2,0},{3,1},{4,6},{5,7},{6,4},{7,5},{8,10},{9,11},{10,... | collective-permute-start | bytes 786440 | tf_op jit(solution)/shard_map/ppermute | solution.py:537
  441.8 39.3 %collective-permute-start.23 = (bf16[2,64,512]{2,1,0:T(8,128)(2,1)S(1)}, bf16[2,64,512]{2,1,0:T(8,128)(2,1)S(1)}, u32[]{:S(2)}, u32[]{:S(2)}) collective-permute-start(bf16[2,64,512]{2,1,0:T(8,128)(2,1)S(1)} %fusion.32), channel_id=1, source_target_pairs={{0,8},{1,9},{2,10},{3,11},{4,12},{5,13},{6,14},{7,15},{8,0},{9,1},... | collective-permute-start | bytes 393224 | tf_op jit(solution)/shard_map/ppermute | solution.py:537
  481.1 131.4 %collective-permute-start.24 = (bf16[1,64,512]{2,1,0:T(8,128)(2,1)S(1)}, bf16[1,64,512]{2,1,0:T(8,128)(2,1)S(1)}, u32[]{:S(2)}, u32[]{:S(2)}) collective-permute-start(bf16[1,64,512]{2,1,0:T(8,128)(2,1)S(1)} %bitcast_add_fusion.11), channel_id=1, source_target_pairs={{0,16},{1,17},{2,18},{3,19},{4,20},{5,21},{6,22},{7,23},{8,24},{9,... | collective-permute-start | bytes 196616 | tf_op jit(solution)/shard_map/ppermute | solution.py:537
  481.2 4.8 copy-start
  486.0 106.1 %collective-permute-start.33 = (bf16[8,176,512]{2,1,0:T(8,128)(2,1)}, bf16[8,176,512]{2,1,0:T(8,128)(2,1)}, u32[]{:S(2)}, u32[]{:S(2)}) collective-permute-start(bf16[8,176,512]{2,1,0:T(8,128)(2,1)} %bitcast.92), channel_id=1, source_target_pairs={{0,4},{1,5},{2,6},{3,7},{4,0},{5,1},{6,2},{7,3},{8,12},{9,13},{10,... | collective-permute-start | bytes 4325384 | tf_op jit(solution)/shard_map/ppermute | solution.py:537
  486.0 6.5 slice-start
  486.0 6.5 slice-start.1
  490.5 132.1 %collective-permute-start.15 = (bf16[8,64,1792]{2,1,0:T(8,128)(2,1)}, bf16[8,64,1792]{2,1,0:T(8,128)(2,1)}, u32[]{:S(2)}, u32[]{:S(2)}) collective-permute-start(bf16[8,64,1792]{2,1,0:T(8,128)(2,1)} %bitcast.55), channel_id=1, source_target_pairs={{0,4},{1,5},{2,6},{3,7},{4,0},{5,1},{6,2},{7,3},{8,12},{9,13},{10,... | collective-permute-start | bytes 5505032 | tf_op jit(solution)/shard_map/ppermute | solution.py:537
  492.5 5.2 copy-start.3
  492.5 5.2 copy-start.13
  497.6 128.3 %collective-permute-start.27 = (bf16[8,64,2816]{2,1,0:T(8,128)(2,1)}, bf16[8,64,2816]{2,1,0:T(8,128)(2,1)}, u32[]{:S(2)}, u32[]{:S(2)}) collective-permute-start(bf16[8,64,2816]{2,1,0:T(8,128)(2,1)} %get-tuple-element.73), channel_id=1, source_target_pairs={{0,2},{1,3},{2,0},{3,1},{4,6},{5,7},{6,4},{7,5},{8,10},{9,11},{10,... | collective-permute-start | bytes 8650760 | tf_op jit(solution)/shard_map/ppermute | solution.py:537
  591.4 4.2 copy-start.4
  594.0 18.5 %collective-permute-start.34 = (bf16[4,176,512]{2,1,0:T(8,128)(2,1)S(1)}, bf16[4,176,512]{2,1,0:T(8,128)(2,1)S(1)}, u32[]{:S(2)}, u32[]{:S(2)}) collective-permute-start(bf16[4,176,512]{2,1,0:T(8,128)(2,1)S(1)} %get-tuple-element.85), channel_id=1, source_target_pairs={{0,2},{1,3},{2,0},{3,1},{4,6},{5,7},{6,4},{7,5},{8,10},{9,11},{10,... | collective-permute-start | bytes 2162696 | tf_op jit(solution)/shard_map/ppermute | solution.py:537
  602.1 20.5 %copy-start.5 = (bf16[4,1,2,64,1792]{4,3,2,1,0:T(8,128)(2,1)S(1)}, bf16[4,1,2,64,1792]{4,3,2,1,0:T(8,128)(2,1)}, u32[]{:S(2)}) copy-start(bf16[4,1,2,64,1792]{4,3,2,1,0:T(8,128)(2,1)} %get-tuple-element.74) | copy-start | bytes 5505028
  612.5 9.9 %collective-permute-start.35 = (bf16[2,176,512]{2,1,0:T(8,128)(2,1)S(1)}, bf16[2,176,512]{2,1,0:T(8,128)(2,1)S(1)}, u32[]{:S(2)}, u32[]{:S(2)}) collective-permute-start(bf16[2,176,512]{2,1,0:T(8,128)(2,1)S(1)} %fusion.29), channel_id=1, source_target_pairs={{0,8},{1,9},{2,10},{3,11},{4,12},{5,13},{6,14},{7,15},{8,0},{9,1},... | collective-permute-start | bytes 1081352 | tf_op jit(solution)/shard_map/ppermute | solution.py:537
  612.7 15.4 %collective-permute-start.25 = (f32[32,512]{1,0:T(8,128)S(1)}, f32[32,512]{1,0:T(8,128)S(1)}, u32[]{:S(2)}, u32[]{:S(2)}) collective-permute-start(f32[32,512]{1,0:T(8,128)S(1)} %dynamic-slice_bitcast_fusion.3), channel_id=1, source_target_pairs={{0,1},{1,0},{2,3},{3,2},{4,5},{5,4},{6,7},{7,6},{8,9},{9,8},{10,11... | collective-permute-start | bytes 196616 | tf_op jit(solution)/shard_map/ppermute | solution.py:537
  622.5 9.9 %collective-permute-start.36 = (bf16[1,176,512]{2,1,0:T(8,128)(2,1)S(1)}, bf16[1,176,512]{2,1,0:T(8,128)(2,1)S(1)}, u32[]{:S(2)}, u32[]{:S(2)}) collective-permute-start(bf16[1,176,512]{2,1,0:T(8,128)(2,1)S(1)} %bitcast_add_fusion.8), channel_id=1, source_target_pairs={{0,16},{1,17},{2,18},{3,19},{4,20},{5,21},{6,22},{7,23},{8,24},{9,... | collective-permute-start | bytes 540680 | tf_op jit(solution)/shard_map/ppermute | solution.py:537
  624.2 20.9 %collective-permute-start.16 = (bf16[4,64,1792]{2,1,0:T(8,128)(2,1)S(1)}, bf16[4,64,1792]{2,1,0:T(8,128)(2,1)S(1)}, u32[]{:S(2)}, u32[]{:S(2)}) collective-permute-start(bf16[4,64,1792]{2,1,0:T(8,128)(2,1)S(1)} %get-tuple-element.83), channel_id=1, source_target_pairs={{0,2},{1,3},{2,0},{3,1},{4,6},{5,7},{6,4},{7,5},{8,10},{9,11},{10,... | collective-permute-start | bytes 2752520 | tf_op jit(solution)/shard_map/ppermute | solution.py:537
  628.0 31.9 %collective-permute-start.28 = (bf16[4,64,2816]{2,1,0:T(8,128)(2,1)S(1)}, bf16[4,64,2816]{2,1,0:T(8,128)(2,1)S(1)}, u32[]{:S(2)}, u32[]{:S(2)}) collective-permute-start(bf16[4,64,2816]{2,1,0:T(8,128)(2,1)S(1)} %get-tuple-element.81), channel_id=1, source_target_pairs={{0,4},{1,5},{2,6},{3,7},{4,0},{5,1},{6,2},{7,3},{8,12},{9,13},{10,... | collective-permute-start | bytes 4325384 | tf_op jit(solution)/shard_map/ppermute | solution.py:537
  632.5 13.5 %collective-permute-start.37 = (f32[88,512]{1,0:T(8,128)S(1)}, f32[88,512]{1,0:T(8,128)S(1)}, u32[]{:S(2)}, u32[]{:S(2)}) collective-permute-start(f32[88,512]{1,0:T(8,128)S(1)} %dynamic-slice_bitcast_fusion.2), channel_id=1, source_target_pairs={{0,1},{1,0},{2,3},{3,2},{4,5},{5,4},{6,7},{7,6},{8,9},{9,8},{10,11... | collective-permute-start | bytes 540680 | tf_op jit(solution)/shard_map/ppermute | solution.py:537
  645.2 10.2 %collective-permute-start.17 = (bf16[2,64,1792]{2,1,0:T(8,128)(2,1)S(1)}, bf16[2,64,1792]{2,1,0:T(8,128)(2,1)S(1)}, u32[]{:S(2)}, u32[]{:S(2)}) collective-permute-start(bf16[2,64,1792]{2,1,0:T(8,128)(2,1)S(1)} %fusion.28), channel_id=1, source_target_pairs={{0,8},{1,9},{2,10},{3,11},{4,12},{5,13},{6,14},{7,15},{8,0},{9,1},... | collective-permute-start | bytes 1376264 | tf_op jit(solution)/shard_map/ppermute | solution.py:537
  655.5 10.3 %collective-permute-start.18 = (bf16[1,64,1792]{2,1,0:T(8,128)(2,1)S(1)}, bf16[1,64,1792]{2,1,0:T(8,128)(2,1)S(1)}, u32[]{:S(2)}, u32[]{:S(2)}) collective-permute-start(bf16[1,64,1792]{2,1,0:T(8,128)(2,1)S(1)} %bitcast_add_fusion.6), channel_id=1, source_target_pairs={{0,16},{1,17},{2,18},{3,19},{4,20},{5,21},{6,22},{7,23},{8,24},{9,... | collective-permute-start | bytes 688136 | tf_op jit(solution)/shard_map/ppermute | solution.py:537
  660.1 18.5 %collective-permute-start.29 = (bf16[2,64,2816]{2,1,0:T(8,128)(2,1)S(1)}, bf16[2,64,2816]{2,1,0:T(8,128)(2,1)S(1)}, u32[]{:S(2)}, u32[]{:S(2)}) collective-permute-start(bf16[2,64,2816]{2,1,0:T(8,128)(2,1)S(1)} %get-tuple-element.87), channel_id=1, source_target_pairs={{0,8},{1,9},{2,10},{3,11},{4,12},{5,13},{6,14},{7,15},{8,0},{9,1},... | collective-permute-start | bytes 2162696 | tf_op jit(solution)/shard_map/ppermute | solution.py:537
  665.9 13.7 %collective-permute-start.19 = (f32[32,1792]{1,0:T(8,128)S(1)}, f32[32,1792]{1,0:T(8,128)S(1)}, u32[]{:S(2)}, u32[]{:S(2)}) collective-permute-start(f32[32,1792]{1,0:T(8,128)S(1)} %dynamic-slice_bitcast_fusion.1), channel_id=1, source_target_pairs={{0,1},{1,0},{2,3},{3,2},{4,5},{5,4},{6,7},{7,6},{8,9},{9,8},{10,11... | collective-permute-start | bytes 688136 | tf_op jit(solution)/shard_map/ppermute | solution.py:537
  678.7 16.6 %collective-permute-start.30 = (bf16[1,64,2816]{2,1,0:T(8,128)(2,1)S(1)}, bf16[1,64,2816]{2,1,0:T(8,128)(2,1)S(1)}, u32[]{:S(2)}, u32[]{:S(2)}) collective-permute-start(bf16[1,64,2816]{2,1,0:T(8,128)(2,1)S(1)} %bitcast_add_fusion.4), channel_id=1, source_target_pairs={{0,16},{1,17},{2,18},{3,19},{4,20},{5,21},{6,22},{7,23},{8,24},{9,... | collective-permute-start | bytes 1081352 | tf_op jit(solution)/shard_map/ppermute | solution.py:537
  695.4 1.7 collective-permute-start.31
